TPU v7x, 256 devices: a whole 4x4x8 slice. The times are simulated.
256 devices in a mesh: tok: 8 (over x, y_lo), feat: 32 (over z, y_hi, core).
Axes of the slice: x: 4, y: 4 (y_hi: 2, y_lo: 2; y = y_hi * 2 + y_lo), z: 8, core: 2. Of those that a mesh axis runs over, the one named last changes fastest.
Arguments:
- query_acts: bfloat16 [2, 384, 8192], P(None, None, 'feat'), may hold values from -6 to 6
- query_grads: bfloat16 [2, 384, 28672], P(None, 'feat', 'tok'), may hold values from -6 to 6
- train_acts: bfloat16 [128, 8192], P(None, 'feat'), may hold values from -6 to 6
- basis_in: bfloat16 [8192, 8192], P('feat', 'tok'), may hold values from -0.0625 to 0.0625
- basis_out: bfloat16 [28672, 28672], P('tok', 'feat'), may hold values from -0.0625 to 0.0625
- eigen_grid: float32 [28672, 8192], P('feat', 'tok'), may hold values from 0.5 to 8
Outputs:
- pulled: bfloat16 [28672, 2, 128], P(('tok', 'feat'))
All inputs are finite; a program needn't handle non-finite values.
Results may differ from a plain program's by a relative error of at most 0.0057.
Values may be sent and summed in bfloat16 or wider, within the bound.
No kernel may reach another device: no remote copies, remote signals or barrier semaphores. Data moves between devices by JAX's collectives and lax.ppermute only.
A program may use at most 64 MiB of HBM per device.

v0:
```python
import jax
import jax.numpy as jnp
from jax import lax
from jax.sharding import PartitionSpec as P


def per_device(query_acts, query_grads, train_acts, basis_in, basis_out, eigen_grid):
    query_count = query_acts.shape[0]
    act_partial = jnp.einsum(
        "qtd,de->qte", query_acts, basis_in, preferred_element_type=jnp.float32
    )
    train_partial = jnp.dot(train_acts, basis_in, preferred_element_type=jnp.float32)
    act_total, train_total = lax.psum((act_partial, train_partial), "feat")
    act_eigen = act_total.astype(jnp.bfloat16)
    train_eigen = train_total.astype(jnp.bfloat16)
    grad_terms = jnp.einsum(
        "qtf,fe->qte",
        lax.all_gather(query_grads, "feat", axis=1, tiled=True),
        basis_out,
        preferred_element_type=jnp.float32,
    )
    grad_eigen = lax.psum(grad_terms, "tok").astype(jnp.bfloat16)
    gram_block = jnp.einsum(
        "qte,qtd->qed", grad_eigen, act_eigen, preferred_element_type=jnp.float32
    )
    precond = gram_block * (1.0 / act_eigen.shape[1]) / eigen_grid
    probe_terms = jnp.einsum(
        "qed,kd->eqk",
        precond,
        train_eigen.astype(jnp.float32),
        preferred_element_type=jnp.float32,
        precision=lax.Precision.HIGHEST,
    )
    probe_eigen = lax.psum(probe_terms, "tok")
    flat_probe = probe_eigen.reshape(probe_eigen.shape[0], -1)
    out_rows = basis_out.shape[0] // lax.axis_size("feat")
    rows_block = basis_out.astype(jnp.float32)
    pulled = lax.psum_scatter(
        jnp.dot(
            rows_block,
            flat_probe,
            preferred_element_type=jnp.float32,
            precision=lax.Precision.HIGHEST,
        ),
        "feat",
        scatter_dimension=0,
        tiled=True,
    )
    return pulled.reshape(out_rows, query_count, -1).astype(jnp.bfloat16)


def solution(mesh):
    placed = (
        P(None, None, "feat"),
        P(None, "feat", "tok"),
        P(None, "feat"),
        P("feat", "tok"),
        P("tok", "feat"),
        P("feat", "tok"),
    )
    return jax.shard_map(
        per_device,
        mesh=mesh,
        in_specs=placed,
        out_specs=P(("tok", "feat"), None, None),
        check_vma=False,
    )
```

profile of v0, /device:TPU:1, one launch (start us, length us, event | category | flops | bytes accessed | tf_op | source)
XLA Modules:
  0.0 527.9 jit_solution(9398291663003329718)
XLA Ops:
  6.5 0.0 copy-start
  6.5 0.0 all-gather.2.cloned.1.call-start
  6.5 0.7 all-gather.2.cloned.1.call-update
  7.3 0.0 all-reduce.5.cloned.1.call-start
  7.3 0.3 copy-done
  7.6 1.1 fusion.14
  8.7 3.2 fusion.9
  11.9 161.3 %all-reduce.7 = (bf16[2,384,1024]{2,1,0:T(8,128)(2,1)S(1)}, bf16[128,1024]{1,0:T(8,128)(2,1)}) all-reduce(f32[2,384,1024]{2,1,0:T(8,128)} %fusion.9, f32[128,1024]{1,0:T(8,128)S(1)} %fusion.14), channel_id=1, replica_groups=mesh['tok'=8,'feat'=32] {'feat'}, use_global_device_ids=true, to_apply=%region_2.0 | all-reduce | flops 917504 | bytes 5505024 | tf_op jit(solution)/shard_map/psum | solution.py:13
  173.2 0.0 all-gather.2.cloned.1.call-done
  173.2 10.8 %fusion.1 = f32[2,384,896]{2,1,0:T(8,128)} fusion(bf16[3584,896]{1,0:T(8,128)(2,1)} %param.10, bf16[2,384,3584]{2,0,1:T(2,128)(2,1)} %all-gather.2.cloned.1.call-done), kind=kOutput, calls=%fused_computation.2 | convolution fusion | flops 4932501504 | bytes 14680064 | tf_op jit(solution)/shard_map/qtf,fe->qte/dot_general | solution.py:16
  184.0 105.2 %all-reduce.6 = bf16[2,384,896]{2,1,0:T(8,128)(2,1)S(1)} all-reduce(f32[2,384,896]{2,1,0:T(8,128)} %fusion.1), channel_id=1, replica_groups=mesh['tok'=8,'feat'=32] {'tok'}, use_global_device_ids=true, to_apply=%region_1.0 | all-reduce | flops 688128 | bytes 4128768 | tf_op jit(solution)/shard_map/psum | solution.py:22
  289.3 0.0 copy-start.1
  289.3 0.0 copy-start.2
  289.3 2.1 fusion.15
  291.4 0.0 copy-done.1
  291.5 0.0 copy-done.2
  291.5 5.8 %fusion = f32[128,2,896]{2,0,1:T(8,128)} fusion(f32[2,896,1024]{2,1,0:T(8,128)S(1)} %fusion.15, f32[896,1024]{1,0:T(8,128)S(1)} %copy-done.1, bf16[128,1024]{1,0:T(8,128)(2,1)S(1)} %copy-done.2), kind=kOutput, calls=%fused_computation.1 | convolution fusion | flops 2822242304 | bytes 12189696 | tf_op jit(solution)/shard_map/qed,kd->eqk/dot_general | solution.py:27
  297.3 0.0 all-reduce.5.cloned.1.call-update
  297.3 0.2 reduce-scatter.4.cloned.1.call-start
  297.5 83.0 %all-reduce.5.cloned.1.call-done = f32[896,256]{0,1:T(8,128)} async-done(((f32[896,256]{0,1:T(8,128)}), f32[896,256]{0,1:T(8,128)}) %all-reduce.5.cloned.1.call-update) | async-done | bytes 917520 | tf_op jit(solution)/shard_map/psum | solution.py:34
  380.5 9.5 %convolution_bitcast_fusion = f32[3584,256]{0,1:T(8,128)} fusion(f32[896,256]{0,1:T(8,128)} %all-reduce.5.cloned.1.call-done, bf16[3584,896]{1,0:T(8,128)(2,1)} %param.10), kind=kOutput, calls=%fused_computation.5 | convolution fusion | flops 9865003008 | bytes 11010048 | tf_op jit(solution)/shard_map/dot_general | solution.py:39
  390.0 5.1 copy.10
  395.2 0.0 reduce-scatter.4.cloned.1.call-update
  395.2 124.4 %reduce-scatter.4.cloned.1.call-done = f32[112,256]{1,0:T(8,128)} async-done(((f32[3584,256]{1,0:T(8,128)}), f32[112,256]{1,0:T(8,128)}) %reduce-scatter.4.cloned.1.call-update) | async-done | bytes 114704
  519.6 1.0 copy.11
  520.6 0.8 copy.8
Async XLA Ops:
  6.5 1.0 copy-start
  6.5 166.7 %all-gather.2.cloned.1.call-start = ((), (), s32[]{:S(2)}) async-start(), calls=%async_computation.1 | async-start | bytes 5677056 | tf_op jit(solution)/shard_map/all_gather | solution.py:18
  7.3 373.2 %all-reduce.5.cloned.1.call-start = ((), (), s32[]{:S(2)}) async-start(), calls=%async_computation.2 | async-start | bytes 1835008 | tf_op jit(solution)/shard_map/psum | solution.py:34
  289.3 2.2 copy-start.1
  289.3 2.2 copy-start.2
  297.3 222.3 %reduce-scatter.4.cloned.1.call-start = ((), (), s32[]{:S(2)}) async-start(), calls=%async_computation.3 | async-start | bytes 3784704
Sparse Core Ops, SparseCore 0:
  10.1 106.7 all-gather.1
  297.4 83.0 all-reduce.4
  395.3 124.2 reduce-scatter.3
where the time goes:
time: 533 us; the launch traced here: 528 us
  blocking collectives  267 us (50%)
  waiting for transfers between devices  208 us (39%)
  matrix products  32.6 us (6%)
  between operations  13.2 us (2%)
  local copies, waits for them, and re-layouts  7.18 us (1%)
    psum x1, blocking collectives, per_device(): act_total, train_total = lax.psum((act_partial, train_partial), 'feat')  161 us
    unnamed x4, waiting for transfers between devices  125 us
    psum x1, blocking collectives, per_device(): grad_eigen = lax.psum(grad_terms, 'tok').astype(jnp.bfloat16)  105 us
    psum x1, waiting for transfers between devices, per_device(): probe_eigen = lax.psum(probe_terms, 'tok')  83 us
    dot_general x1, matrix products, per_device(): jnp.einsum('qtf,fe->qte', lax.all_gather(query_grads, 'feat', axis=1, til...  10.8 us
  transfers between devices with their start and end apart: 3, of which 2 were waited for; matrix products, arithmetic and copies ran while one was open for 1% of the time, Pallas kernels for 0%

commit v1 on v0

v1 whole, which is shorter than its diff:
```python
import jax
import jax.numpy as jnp
from jax import lax
from jax.sharding import Mesh, PartitionSpec as P

BF16 = jnp.bfloat16
F32 = jnp.float32
SIZES = {"x": 4, "ylo": 2, "z": 8, "yhi": 2, "core": 2}
TOK = ("x", "ylo")
FEAT = ("z", "yhi", "core")


def swap(array, axis):
    return lax.ppermute(array, axis, [(0, 1), (1, 0)])


def pick(array, index, axis=0):
    return lax.dynamic_index_in_dim(array, index, axis, keepdims=False)


def exchange(pieces, axes):
    return lax.all_to_all(pieces, axes, 0, 0)


def scatter_sum(pieces, axes):
    return exchange(pieces.astype(BF16), axes).astype(F32).sum(axis=0)


def gather(block, axes, count):
    return exchange(jnp.broadcast_to(block[None], (count,) + block.shape), axes)


def direct_gather(own):
    blocks = {(0, 0): own}
    for i, j in ((2, 1), (2, 0), (1, 1), (3, 1), (1, 0), (3, 0), (0, 1)):
        pairs = [
            ((a + i) % 4 * 2 + (b + j) % 2, a * 2 + b) for a in range(4) for b in range(2)
        ]
        blocks[i, j] = lax.ppermute(own, TOK, pairs)
    return jnp.stack([blocks[i, j] for i in range(4) for j in range(2)])


def roll_blocks(array, by):
    twice = jnp.concatenate([array, array], axis=0)
    return lax.dynamic_slice_in_dim(twice, by, array.shape[0], 0)


def in_order(own, index, axis):
    other = swap(own, axis)
    return jnp.where(index == 0, own, other), jnp.where(index == 0, other, own)


def per_device(query_acts, query_grads, train_acts, basis_in, basis_out, eigen_grid):
    x, ylo, yhi, core = (lax.axis_index(a) for a in ("x", "ylo", "yhi", "core"))

    acts = query_acts.reshape(2, 8, 2, 2, 12, 256).transpose(3, 1, 2, 0, 4, 5)
    acts = jnp.concatenate(
        [acts.reshape(2, 8, 48, 256), train_acts.reshape(2, 8, 8, 256)], axis=2
    ).reshape(2, 448, 256)
    give_acts, keep_acts = pick(acts, 1 - core), pick(acts, core)
    give_cols = lax.dynamic_slice_in_dim(basis_in, (1 - yhi) * 512, 512, 1)
    keep_cols = lax.dynamic_slice_in_dim(basis_in, yhi * 512, 512, 1)
    dot = lambda a, b: jnp.dot(a, b, preferred_element_type=F32)

    give, keep = dot(give_acts, give_cols), dot(give_acts, keep_cols)

    own = query_grads.reshape(24, 3584)
    both = in_order(own, yhi, "yhi")
    both, give, keep = lax.optimization_barrier((both, give, keep))
    near_grads = lax.all_gather(jnp.concatenate(both), "z", axis=0, tiled=True)

    give = swap(give, "core") + dot(keep_acts, give_cols)
    keep = swap(keep, "core") + dot(keep_acts, keep_cols)
    pair = keep + swap(give.astype(BF16), "yhi").astype(F32)
    rows = basis_out.reshape(16, 2, 112, 896)
    give_rows = pick(rows, 1 - core, 1).reshape(1792, 896)
    keep_rows = pick(rows, core, 1).reshape(1792, 896)
    pair, give_rows, keep_rows = lax.optimization_barrier((pair, give_rows, keep_rows))
    mine = scatter_sum(pair.reshape(8, 56, 512), "z").astype(BF16)
    mine = jnp.concatenate(in_order(mine, yhi, "yhi"), axis=1)
    near_grads, mine = lax.optimization_barrier((near_grads, mine))
    mine = jnp.concatenate([mine, jnp.zeros((40, 1024), BF16)], axis=0)
    near_rotated = lax.all_gather(mine, "z", axis=0)

    far_grads = swap(near_grads, "core")
    near = dot(near_grads, basis_out).astype(BF16)
    far = dot(far_grads, basis_out).astype(BF16)
    pieces = jnp.concatenate([near, far], axis=0)
    summed = scatter_sum(pieces.reshape(8, 96, 896), TOK).astype(BF16)
    grad = direct_gather(summed)
    near_rotated, _ = lax.optimization_barrier((near_rotated, summed))
    near_rotated = near_rotated[:, :56].reshape(448, 1024)

    rotated = jnp.concatenate([near_rotated, swap(near_rotated, "core")], axis=0)
    train = rotated.reshape(2, 8, 56, 1024)[:, :, 48:].reshape(2, 64, 1024)
    train = jnp.where(core == 0, train, train[::-1]).reshape(128, 1024)
    rotated = rotated.reshape(4, 2, 112, 1024)
    rotated = jnp.where(ylo == 0, rotated, rotated[:, ::-1])
    rotated = roll_blocks(rotated, x).reshape(896, 1024)
    grad, rotated, train = lax.optimization_barrier((grad, rotated, train))
    grad = jnp.pad(grad.reshape(16, 48, 896), ((0, 0), (0, 8), (0, 0)))
    row = jnp.arange(56)
    of_query = (row // 12 % 2)[None, :] == jnp.arange(2)[:, None]
    grad = jnp.where(of_query[:, None, :, None], grad[None], 0).reshape(2, 896, 896)

    gram = jnp.einsum("qte,td->qed", grad, rotated, preferred_element_type=F32)
    precond = gram * (1.0 / 384) / eigen_grid
    probe = jnp.einsum(
        "qed,kd->eqk", precond.astype(BF16), train, preferred_element_type=F32
    )
    probe = scatter_sum(probe.reshape(8, 112, 256), TOK).astype(BF16)
    probe = gather(probe, TOK, 8).reshape(896, 256)

    chip = swap(dot(give_rows, probe).astype(BF16), "core").astype(F32)
    chip = (dot(keep_rows, probe) + chip).reshape(16, 112, 256)
    pulled = scatter_sum(chip, ("z", "yhi"))
    return pulled.astype(BF16).reshape(112, 2, 128)


def solution(mesh):
    grid = Mesh(mesh.devices.reshape(tuple(SIZES.values())), tuple(SIZES))
    placed = (
        P(None, None, FEAT),
        P(None, FEAT, TOK),
        P(None, FEAT),
        P(FEAT, TOK),
        P(TOK, FEAT),
        P(FEAT, TOK),
    )
    return jax.shard_map(
        per_device,
        mesh=grid,
        in_specs=placed,
        out_specs=P(TOK + FEAT, None, None),
        check_vma=False,
    )
```

time: 533 us -> 221 us (0.41)
  blocking collectives: 267 us -> 80.9 us
  waiting for transfers between devices: 208 us -> 40 us
  starting transfers between devices: 0.26 us -> 36.9 us
  local copies, waits for them, and re-layouts: 7.18 us -> 15.2 us
  other arithmetic: 0 us -> 6.64 us
  matrix products: 32.6 us -> 26.6 us
    psum x2 -> x0, blocking collectives: 267 us -> none  [the longest x1 161 us: per_device(): act_total, train_total = lax.psum((act_partial, train_partial), 'feat')]
    unnamed x4 -> x2, waiting for transfers between devices: 125 us -> 0.03 us
    psum x1 -> x0, waiting for transfers between devices: 83 us -> none  [per_device(): probe_eigen = lax.psum(probe_terms, 'tok')]
    all_to_all x0 -> x4, blocking collectives: none -> 80.9 us  [exchange(): return lax.all_to_all(pieces, axes, 0, 0)]
    ppermute x0 -> x15, starting transfers between devices: none -> 32 us  [the longest x8 23.8 us: swap(): return lax.ppermute(array, axis, [(0, 1), (1, 0)])]
    all_to_all x0 -> x1, waiting for transfers between devices: none -> 21.2 us  [exchange(): return lax.all_to_all(pieces, axes, 0, 0)]
    ppermute x0 -> x15, waiting for transfers between devices: none -> 17.3 us  [the longest x8 11.5 us: swap(): return lax.ppermute(array, axis, [(0, 1), (1, 0)])]
    dynamic_slice x0 -> x1, local copies, waits for them, and re-layouts: none -> 6.09 us  [pick(): return lax.dynamic_index_in_dim(array, index, axis, keepdims=False)]
  transfers between devices with their start and end apart: 3 -> 18, of which waited for: 2 -> 9; matrix products, arithmetic and copies ran while one was open for 1% -> 12% of each run, Pallas kernels for 0% -> 0%
where the time goes in v1:
time: 221 us; the launch traced here: 220 us
  blocking collectives  80.9 us (37%)
  waiting for transfers between devices  40 us (18%)
  starting transfers between devices  36.9 us (17%)
  matrix products  26.6 us (12%)
  local copies, waits for them, and re-layouts  15.2 us (7%)
  between operations  13.8 us (6%)
  other arithmetic  6.64 us (3%)
    all_to_all x4, blocking collectives, exchange(): return lax.all_to_all(pieces, axes, 0, 0)  80.9 us
    ppermute x8, starting transfers between devices, swap(): return lax.ppermute(array, axis, [(0, 1), (1, 0)])  23.8 us
    all_to_all x1, waiting for transfers between devices, exchange(): return lax.all_to_all(pieces, axes, 0, 0)  21.2 us
    dot_general x8, matrix products, per_device(): dot = lambda a, b: jnp.dot(a, b, preferred_element_type=F32)  18.2 us
    ppermute x8, waiting for transfers between devices, swap(): return lax.ppermute(array, axis, [(0, 1), (1, 0)])  11.5 us
    dot_general x1, matrix products, per_device(): jnp.einsum('qed,kd->eqk', precond.astype(BF16), train, preferred_element_...  8.35 us
    ppermute x7, starting transfers between devices, direct_gather(): blocks[i, j] = lax.ppermute(own, TOK, pairs)  8.22 us
    dynamic_slice x1, local copies, waits for them, and re-layouts, pick(): return lax.dynamic_index_in_dim(array, index, axis, keepdims=False)  6.09 us
  transfers between devices with their start and end apart: 18, of which 9 were waited for; matrix products, arithmetic and copies ran while one was open for 12% of the time, Pallas kernels for 0%

profile of v1, /device:TPU:1, one launch (start us, length us, event | category | flops | bytes accessed | tf_op | source)
XLA Modules:
  0.0 220.1 jit_solution(6388679929378945070)
XLA Ops:
  6.5 1.0 copy.24
  7.6 3.8 %collective-permute-start = (bf16[24,3584]{1,0:T(8,128)(2,1)S(1)}, bf16[24,3584]{1,0:T(8,128)(2,1)S(1)}, u32[]{:S(2)}, u32[]{:S(2)}) collective-permute-start(bf16[24,3584]{1,0:T(8,128)(2,1)S(1)} %reshape.111), channel_id=1, source_target_pairs={{0,2},{2,0},{1,3},{3,1},{4,6},{6,4},{5,7},{7,5},{8,10},{10,8},{9,1... | collective-permute-start | bytes 516104 | tf_op jit(solution)/shard_map/ppermute | solution.py:14
  11.4 1.4 copy.25
  12.8 0.2 copy.26
  13.2 0.1 copy.28
  13.3 0.3 fusion.32
  13.6 0.3 fusion.28
  13.9 0.6 collective-permute-done
  14.5 0.8 pad_maximum_fusion.3
  15.3 0.0 all-gather.4.cloned.1.call-update
  15.3 0.0 all-gather.6.cloned.1.call-start
  15.4 3.5 %collective-permute-start.2 = (f32[448,512]{1,0:T(8,128)S(1)}, f32[448,512]{1,0:T(8,128)}, u32[]{:S(2)}, u32[]{:S(2)}) collective-permute-start(f32[448,512]{1,0:T(8,128)S(1)} %fusion.32), channel_id=1, source_target_pairs={{0,1},{1,0},{2,3},{3,2},{4,5},{5,4},{6,7},{7,6},{8,9},{9,8},{10,11... | collective-permute-start | bytes 2752520 | tf_op jit(solution)/shard_map/ppermute | solution.py:14
  18.8 0.1 collective-permute-start.1
  18.9 2.1 collective-permute-done.2
  21.0 1.5 add_convert_fusion.1
  22.5 2.0 collective-permute-start.3
  24.5 0.3 fusion.26
  24.8 6.1 %constant_dynamic-slice_fusion = (bf16[16,1,112,896]{3,2,1,0:T(8,128)(2,1)}, bf16[16,1,112,896]{3,2,1,0:T(8,128)(2,1)}) fusion(bf16[16,2,112,896]{3,2,1,0:T(8,128)(2,1)} %bitcast.76, s32[]{:T(128)S(6)} %select_n.90, s32[]{:T(128)S(6)} %select_n.87), kind=kLoop, calls=%fused_computation.58 | loop fusion | bytes 12845064 | tf_op jit(solution)/shard_map/jit(dynamic_index_in_dim)/dynamic_slice | solution.py:18
  30.9 5.0 %collective-permute-done.3 = bf16[448,512]{1,0:T(8,128)(2,1)S(1)} collective-permute-done((bf16[448,512]{1,0:T(8,128)(2,1)S(1)}, bf16[448,512]{1,0:T(8,128)(2,1)S(1)}, u32[]{:S(2)}, u32[]{:S(2)}) %collective-permute-start.3) | collective-permute-done | bytes 458784 | tf_op jit(solution)/shard_map/ppermute | solution.py:14
  35.8 1.5 convert_add_fusion
  37.3 27.1 %all_to_all.25 = bf16[8,56,512]{2,1,0:T(8,128)(2,1)S(1)} all-to-all(bf16[8,56,512]{2,1,0:T(8,128)(2,1)S(1)} %bitcast.89), channel_id=1, replica_groups=mesh['x'=4,'ylo'=2,'z'=8,'yhi'=2,'core'=2] {'z'}, dimensions={0} | all-to-all | bytes 917504 | tf_op jit(solution)/shard_map/all_to_all | solution.py:22
  64.4 0.1 reduce_sum.48
  64.4 3.2 %collective-permute-start.4 = (bf16[56,512]{1,0:T(8,128)(2,1)S(1)}, bf16[56,512]{1,0:T(8,128)(2,1)S(1)}, u32[]{:S(2)}, u32[]{:S(2)}) collective-permute-start(bf16[56,512]{1,0:T(8,128)(2,1)S(1)} %reduce_sum.48), channel_id=1, source_target_pairs={{0,2},{2,0},{1,3},{3,1},{4,6},{6,4},{5,7},{7,5},{8,10},{10,8},{9,1... | collective-permute-start | bytes 172040 | tf_op jit(solution)/shard_map/ppermute | solution.py:14
  67.6 1.6 collective-permute-done.4
  69.3 0.0 slice-start
  69.3 1.6 all-gather.4.cloned.1.call-done
  70.9 2.8 %collective-permute-start.5 = (bf16[384,3584]{1,0:T(8,128)(2,1)}, bf16[384,3584]{1,0:T(8,128)(2,1)}, u32[]{:S(2)}, u32[]{:S(2)}) collective-permute-start(bf16[384,3584]{1,0:T(8,128)(2,1)} %all-gather.4.cloned.1.call-done), channel_id=1, source_target_pairs={{0,1},{1,0},{2,3},{3,2},{4,5},{5,4},{6,7},{7,6},{8,9},{9,8},{10,11... | collective-permute-start | bytes 8257544 | tf_op jit(solution)/shard_map/ppermute | solution.py:14
  73.7 0.7 concatenate.25
  74.3 0.0 all-gather.6.cloned.1.call-update
  74.4 6.8 %convolution_convert_fusion.2 = bf16[384,896]{1,0:T(8,128)(2,1)S(1)} fusion(bf16[384,3584]{1,0:T(8,128)(2,1)} %all-gather.4.cloned.1.call-done, bf16[3584,896]{1,0:T(8,128)(2,1)} %param.10), kind=kOutput, calls=%fused_computation.17 | convolution fusion | flops 2466594816 | bytes 9863168 | tf_op jit(solution)/shard_map/dot_general | solution.py:63
  81.2 4.8 %convolution_convert_fusion.1 = bf16[384,896]{1,0:T(8,128)(2,1)S(1)} fusion(bf16[384,3584]{1,0:T(8,128)(2,1)} %collective-permute-done.5, bf16[3584,896]{1,0:T(8,128)(2,1)S(1)} %bitcast.78), kind=kOutput, calls=%fused_computation.16 | convolution fusion | flops 2466594816 | bytes 9863168 | tf_op jit(solution)/shard_map/dot_general | solution.py:63
  86.0 1.2 pad_maximum_fusion.1
  87.2 4.9 %all-to-all-start.1 = ((bf16[8,96,896]{2,1,0:T(8,128)(2,1)}), bf16[8,96,896]{2,1,0:T(8,128)(2,1)S(1)}, u32[]{:S(2)}, u32[]{:S(2)}) async-start(bf16[8,96,896]{2,1,0:T(8,128)(2,1)} %bitcast.11), calls=%async_computation.1 | async-start | bytes 2752512 | tf_op jit(solution)/shard_map/all_to_all | solution.py:22
  92.1 0.1 broadcast_in_dim.39
  92.2 21.2 %all-to-all-done.1 = bf16[8,96,896]{2,1,0:T(8,128)(2,1)S(1)} async-done(((bf16[8,96,896]{2,1,0:T(8,128)(2,1)}), bf16[8,96,896]{2,1,0:T(8,128)(2,1)S(1)}, u32[]{:S(2)}, u32[]{:S(2)}) %all-to-all-start.1) | async-done | bytes 1376288 | tf_op jit(solution)/shard_map/all_to_all | solution.py:22
  113.4 0.2 reduce_sum.49
  113.6 0.7 collective-permute-start.6
  114.3 1.2 collective-permute-start.8
  115.5 2.6 %collective-permute-start.9 = (bf16[96,896]{1,0:T(8,128)(2,1)S(1)}, bf16[96,896]{1,0:T(8,128)(2,1)S(1)}, u32[]{:S(2)}, u32[]{:S(2)}) collective-permute-start(bf16[96,896]{1,0:T(8,128)(2,1)S(1)} %reduce_sum.49), channel_id=1, source_target_pairs={{128,0},{160,32},{192,64},{224,96},{0,128},{32,160},{64,192},{96,2... | collective-permute-start | bytes 516104 | tf_op jit(solution)/shard_map/ppermute | solution.py:39
  118.1 0.3 collective-permute-start.10
  118.4 1.2 slice.6
  119.7 1.3 collective-permute-start.11
  121.0 2.1 collective-permute-start.12
  123.2 4.6 %collective-permute-start.13 = (bf16[448,1024]{1,0:T(8,128)(2,1)S(1)}, bf16[448,1024]{1,0:T(8,128)(2,1)S(1)}, u32[]{:S(2)}, u32[]{:S(2)}) collective-permute-start(bf16[448,1024]{1,0:T(8,128)(2,1)S(1)} %bitcast.84), channel_id=1, source_target_pairs={{0,1},{1,0},{2,3},{3,2},{4,5},{5,4},{6,7},{7,6},{8,9},{9,8},{10,11... | collective-permute-start | bytes 2752520 | tf_op jit(solution)/shard_map/ppermute | solution.py:14
  127.8 2.2 %collective-permute-done.11 = bf16[96,896]{1,0:T(8,128)(2,1)S(1)} collective-permute-done((bf16[96,896]{1,0:T(8,128)(2,1)S(1)}, bf16[96,896]{1,0:T(8,128)(2,1)S(1)}, u32[]{:S(2)}, u32[]{:S(2)}) %collective-permute-start.11) | collective-permute-done | bytes 172064 | tf_op jit(solution)/shard_map/ppermute | solution.py:39
  130.1 3.6 %collective-permute-done.12 = bf16[96,896]{1,0:T(8,128)(2,1)S(1)} collective-permute-done((bf16[96,896]{1,0:T(8,128)(2,1)S(1)}, bf16[96,896]{1,0:T(8,128)(2,1)S(1)}, u32[]{:S(2)}, u32[]{:S(2)}) %collective-permute-start.12) | collective-permute-done | bytes 172064 | tf_op jit(solution)/shard_map/ppermute | solution.py:39
  133.7 0.1 pad_maximum_fusion
  133.9 0.5 reverse_select_fusion
  134.4 1.9 fusion.8
  136.4 0.1 pad.5
  136.5 2.4 %copy.29 = bf16[896,896]{0,1:T(8,128)(2,1)} copy(bf16[896,896]{1,0:T(8,128)(2,1)S(1)} %bitcast.79) | data formatting | bytes 3211264 | tf_op jit(solution)/shard_map/jit(_where)/broadcast_in_dim | solution.py:104
  138.9 8.3 %fusion.20 = bf16[896,2,128]{0,2,1:T(8,128)(2,1)S(1)} fusion(f32[896,1024]{1,0:T(8,128)} %param.11, pred[2,896]{1,0:T(4,128)(4,1)S(1)} %broadcast_in_dim.39, bf16[896,1024]{1,0:T(8,128)(2,1)} %bitcast.88, bf16[896,896]{0,1:T(8,128)(2,1)} %copy.29, bf16[128,1024]{1,0:T(8,128)(2,1)S(1)} %bitcast.97), kind=kOutput, calls=%fused_computation.19 | convolution fusion | flops 3765436416 | bytes 7833344 | tf_op jit(solution)/shard_map/qed,kd->eqk/dot_general | solution.py:108
  147.3 0.6 reshape.132
  147.8 0.3 copy.31
  148.2 12.3 %all_to_all.26 = bf16[8,112,256]{2,1,0:T(8,128)(2,1)S(1)} all-to-all(bf16[8,112,256]{2,1,0:T(8,128)(2,1)S(1)} %copy.31), channel_id=1, replica_groups=mesh['x'=4,'ylo'=2,'z'=8,'yhi'=2,'core'=2] {'x','ylo'}, dimensions={0} | all-to-all | bytes 917504 | tf_op jit(solution)/shard_map/all_to_all | solution.py:22
  160.5 0.1 reduce_sum.50
  160.6 9.6 %all_to_all.27 = bf16[8,112,256]{2,1,0:T(8,128)(2,1)S(1)} all-to-all(bf16[8,112,256]{2,1,0:T(8,128)(2,1)S(1)} %broadcast_in_dim.44), channel_id=1, replica_groups=mesh['x'=4,'ylo'=2,'z'=8,'yhi'=2,'core'=2] {'x','ylo'}, dimensions={0} | all-to-all | bytes 917504 | tf_op jit(solution)/shard_map/all_to_all | solution.py:22
  170.2 3.2 %convolution_convert_fusion = bf16[1792,256]{1,0:T(8,128)(2,1)S(1)} fusion(bf16[1792,896]{1,0:T(8,128)(2,1)} %bitcast.87, bf16[896,256]{1,0:T(8,128)(2,1)S(1)} %bitcast.95), kind=kOutput, calls=%fused_computation.8 | convolution fusion | flops 822542336 | bytes 4587520 | tf_op jit(solution)/shard_map/dot_general | solution.py:63
  173.4 3.8 %collective-permute-start.14 = (bf16[1792,256]{1,0:T(8,128)(2,1)S(1)}, bf16[1792,256]{1,0:T(8,128)(2,1)S(1)}, u32[]{:S(2)}, u32[]{:S(2)}) collective-permute-start(bf16[1792,256]{1,0:T(8,128)(2,1)S(1)} %convolution_convert_fusion), channel_id=1, source_target_pairs={{0,1},{1,0},{2,3},{3,2},{4,5},{5,4},{6,7},{7,6},{8,9},{9,8},{10,11... | collective-permute-start | bytes 2752520 | tf_op jit(solution)/shard_map/ppermute | solution.py:14
  177.2 2.1 collective-permute-done.14
  179.3 1.2 add_convert_fusion
  180.5 31.9 %all_to_all.28 = bf16[16,112,256]{2,1,0:T(8,128)(2,1)S(1)} all-to-all(bf16[16,112,256]{2,1,0:T(8,128)(2,1)S(1)} %bitcast.93), channel_id=1, replica_groups=mesh['x'=4,'ylo'=2,'z'=8,'yhi'=2,'core'=2] {'z','yhi'}, dimensions={0} | all-to-all | bytes 1835008 | tf_op jit(solution)/shard_map/all_to_all | solution.py:22
  212.4 0.1 reduce_sum.51
  212.6 0.6 reshape.128
  (41 shorter events, 0.5 us)
Async XLA Ops:
  6.5 6.7 %copy-start = (bf16[256,1024]{1,0:T(8,128)(2,1)S(1)}, bf16[256,1024]{1,0:T(8,128)(2,1)}, u32[]{:S(2)}) copy-start(bf16[256,1024]{1,0:T(8,128)(2,1)} %param.9) | copy-start | bytes 1572868
  6.5 6.5 %copy-start.2 = (bf16[128,256]{1,0:T(8,128)(2,1)S(1)}, bf16[128,256]{1,0:T(8,128)(2,1)}, u32[]{:S(2)}) copy-start(bf16[128,256]{1,0:T(8,128)(2,1)} %param.8) | copy-start | bytes 196612
  6.5 64.3 %all-gather.4.cloned.1.call-start = ((), (), s32[]{:S(2)}) async-start(), calls=%async_computation.5 | async-start | bytes 3096576 | tf_op jit(solution)/shard_map/all_gather | solution.py:70
  7.6 6.9 %collective-permute-start = (bf16[24,3584]{1,0:T(8,128)(2,1)S(1)}, bf16[24,3584]{1,0:T(8,128)(2,1)S(1)}, u32[]{:S(2)}, u32[]{:S(2)}) collective-permute-start(bf16[24,3584]{1,0:T(8,128)(2,1)S(1)} %reshape.111), channel_id=1, source_target_pairs={{0,2},{2,0},{1,3},{3,1},{4,6},{6,4},{5,7},{7,5},{8,10},{10,8},{9,1... | collective-permute-start | bytes 516104 | tf_op jit(solution)/shard_map/ppermute | solution.py:14
  15.3 103.1 %all-gather.6.cloned.1.call-start = ((), (), s32[]{:S(2)}) async-start(), calls=%async_computation.6 | async-start | bytes 1769472 | tf_op jit(solution)/shard_map/all_gather | solution.py:83
  15.4 5.7 %collective-permute-start.2 = (f32[448,512]{1,0:T(8,128)S(1)}, f32[448,512]{1,0:T(8,128)}, u32[]{:S(2)}, u32[]{:S(2)}) collective-permute-start(f32[448,512]{1,0:T(8,128)S(1)} %fusion.32), channel_id=1, source_target_pairs={{0,1},{1,0},{2,3},{3,2},{4,5},{5,4},{6,7},{7,6},{8,9},{9,8},{10,11... | collective-permute-start | bytes 2752520 | tf_op jit(solution)/shard_map/ppermute | solution.py:14
  18.8 12.0 %collective-permute-start.1 = (f32[448,512]{1,0:T(8,128)S(1)}, f32[448,512]{1,0:T(8,128)}, u32[]{:S(2)}, u32[]{:S(2)}) collective-permute-start(f32[448,512]{1,0:T(8,128)S(1)} %fusion.28), channel_id=1, source_target_pairs={{0,1},{1,0},{2,3},{3,2},{4,5},{5,4},{6,7},{7,6},{8,9},{9,8},{10,11... | collective-permute-start | bytes 2752520 | tf_op jit(solution)/shard_map/ppermute | solution.py:14
  22.5 13.3 %collective-permute-start.3 = (bf16[448,512]{1,0:T(8,128)(2,1)S(1)}, bf16[448,512]{1,0:T(8,128)(2,1)S(1)}, u32[]{:S(2)}, u32[]{:S(2)}) collective-permute-start(bf16[448,512]{1,0:T(8,128)(2,1)S(1)} %add_convert_fusion.1), channel_id=1, source_target_pairs={{0,2},{2,0},{1,3},{3,1},{4,6},{6,4},{5,7},{7,5},{8,10},{10,8},{9,1... | collective-permute-start | bytes 1376264 | tf_op jit(solution)/shard_map/ppermute | solution.py:14
  64.4 4.8 %collective-permute-start.4 = (bf16[56,512]{1,0:T(8,128)(2,1)S(1)}, bf16[56,512]{1,0:T(8,128)(2,1)S(1)}, u32[]{:S(2)}, u32[]{:S(2)}) collective-permute-start(bf16[56,512]{1,0:T(8,128)(2,1)S(1)} %reduce_sum.48), channel_id=1, source_target_pairs={{0,2},{2,0},{1,3},{3,1},{4,6},{6,4},{5,7},{7,5},{8,10},{10,8},{9,1... | collective-permute-start | bytes 172040 | tf_op jit(solution)/shard_map/ppermute | solution.py:14
  69.3 11.9 %slice-start = ((s8[6422528]{0:T(1024)(128)(4,1)}), s8[2228224]{0:T(1024)(128)(4,1)S(1)}, s32[]{:S(2)}) async-start(s8[6422528]{0:T(1024)(128)(4,1)} %bitcast.77), calls=%async_computation.7 | async-start | bytes 4456448
  70.9 10.3 %collective-permute-start.5 = (bf16[384,3584]{1,0:T(8,128)(2,1)}, bf16[384,3584]{1,0:T(8,128)(2,1)}, u32[]{:S(2)}, u32[]{:S(2)}) collective-permute-start(bf16[384,3584]{1,0:T(8,128)(2,1)} %all-gather.4.cloned.1.call-done), channel_id=1, source_target_pairs={{0,1},{1,0},{2,3},{3,2},{4,5},{5,4},{6,7},{7,6},{8,9},{9,8},{10,11... | collective-permute-start | bytes 8257544 | tf_op jit(solution)/shard_map/ppermute | solution.py:14
  74.4 6.8 %slice-start.1 = ((s8[6422528]{0:T(1024)(128)(4,1)}), s8[4194304]{0:T(1024)(128)(4,1)S(1)}, s32[]{:S(2)}) async-start(s8[6422528]{0:T(1024)(128)(4,1)} %bitcast.77), calls=%async_computation.8 | async-start | bytes 8388608
  87.2 26.2 %all-to-all-start.1 = ((bf16[8,96,896]{2,1,0:T(8,128)(2,1)}), bf16[8,96,896]{2,1,0:T(8,128)(2,1)S(1)}, u32[]{:S(2)}, u32[]{:S(2)}) async-start(bf16[8,96,896]{2,1,0:T(8,128)(2,1)} %bitcast.11), calls=%async_computation.1 | async-start | bytes 2752512 | tf_op jit(solution)/shard_map/all_to_all | solution.py:22
  113.6 6.1 %collective-permute-start.6 = (bf16[96,896]{1,0:T(8,128)(2,1)S(1)}, bf16[96,896]{1,0:T(8,128)(2,1)S(1)}, u32[]{:S(2)}, u32[]{:S(2)}) collective-permute-start(bf16[96,896]{1,0:T(8,128)(2,1)S(1)} %reduce_sum.49), channel_id=1, source_target_pairs={{32,0},{0,32},{96,64},{64,96},{160,128},{128,160},{224,192},{192,2... | collective-permute-start | bytes 516104 | tf_op jit(solution)/shard_map/ppermute | solution.py:39
  114.3 6.7 %collective-permute-start.7 = (bf16[96,896]{1,0:T(8,128)(2,1)S(1)}, bf16[96,896]{1,0:T(8,128)(2,1)S(1)}, u32[]{:S(2)}, u32[]{:S(2)}) collective-permute-start(bf16[96,896]{1,0:T(8,128)(2,1)S(1)} %reduce_sum.49), channel_id=1, source_target_pairs={{64,0},{96,32},{128,64},{160,96},{192,128},{224,160},{0,192},{32,2... | collective-permute-start | bytes 516104 | tf_op jit(solution)/shard_map/ppermute | solution.py:39
  114.3 8.9 %collective-permute-start.8 = (bf16[96,896]{1,0:T(8,128)(2,1)S(1)}, bf16[96,896]{1,0:T(8,128)(2,1)S(1)}, u32[]{:S(2)}, u32[]{:S(2)}) collective-permute-start(bf16[96,896]{1,0:T(8,128)(2,1)S(1)} %reduce_sum.49), channel_id=1, source_target_pairs={{96,0},{64,32},{160,64},{128,96},{224,128},{192,160},{32,192},{0,2... | collective-permute-start | bytes 516104 | tf_op jit(solution)/shard_map/ppermute | solution.py:39
  115.5 12.3 %collective-permute-start.9 = (bf16[96,896]{1,0:T(8,128)(2,1)S(1)}, bf16[96,896]{1,0:T(8,128)(2,1)S(1)}, u32[]{:S(2)}, u32[]{:S(2)}) collective-permute-start(bf16[96,896]{1,0:T(8,128)(2,1)S(1)} %reduce_sum.49), channel_id=1, source_target_pairs={{128,0},{160,32},{192,64},{224,96},{0,128},{32,160},{64,192},{96,2... | collective-permute-start | bytes 516104 | tf_op jit(solution)/shard_map/ppermute | solution.py:39
  118.1 9.7 %collective-permute-start.10 = (bf16[96,896]{1,0:T(8,128)(2,1)S(1)}, bf16[96,896]{1,0:T(8,128)(2,1)S(1)}, u32[]{:S(2)}, u32[]{:S(2)}) collective-permute-start(bf16[96,896]{1,0:T(8,128)(2,1)S(1)} %reduce_sum.49), channel_id=1, source_target_pairs={{160,0},{128,32},{224,64},{192,96},{32,128},{0,160},{96,192},{64,2... | collective-permute-start | bytes 516104 | tf_op jit(solution)/shard_map/ppermute | solution.py:39
  119.7 10.3 %collective-permute-start.11 = (bf16[96,896]{1,0:T(8,128)(2,1)S(1)}, bf16[96,896]{1,0:T(8,128)(2,1)S(1)}, u32[]{:S(2)}, u32[]{:S(2)}) collective-permute-start(bf16[96,896]{1,0:T(8,128)(2,1)S(1)} %reduce_sum.49), channel_id=1, source_target_pairs={{192,0},{224,32},{0,64},{32,96},{64,128},{96,160},{128,192},{160,2... | collective-permute-start | bytes 516104 | tf_op jit(solution)/shard_map/ppermute | solution.py:39
  121.0 12.6 %collective-permute-start.12 = (bf16[96,896]{1,0:T(8,128)(2,1)S(1)}, bf16[96,896]{1,0:T(8,128)(2,1)S(1)}, u32[]{:S(2)}, u32[]{:S(2)}) collective-permute-start(bf16[96,896]{1,0:T(8,128)(2,1)S(1)} %reduce_sum.49), channel_id=1, source_target_pairs={{224,0},{192,32},{32,64},{0,96},{96,128},{64,160},{160,192},{128,2... | collective-permute-start | bytes 516104 | tf_op jit(solution)/shard_map/ppermute | solution.py:39
  123.2 10.5 %collective-permute-start.13 = (bf16[448,1024]{1,0:T(8,128)(2,1)S(1)}, bf16[448,1024]{1,0:T(8,128)(2,1)S(1)}, u32[]{:S(2)}, u32[]{:S(2)}) collective-permute-start(bf16[448,1024]{1,0:T(8,128)(2,1)S(1)} %bitcast.84), channel_id=1, source_target_pairs={{0,1},{1,0},{2,3},{3,2},{4,5},{5,4},{6,7},{7,6},{8,9},{9,8},{10,11... | collective-permute-start | bytes 2752520 | tf_op jit(solution)/shard_map/ppermute | solution.py:14
  170.2 9.1 %copy-start.1 = (bf16[16,1,112,896]{3,2,1,0:T(8,128)(2,1)S(1)}, bf16[16,1,112,896]{3,2,1,0:T(8,128)(2,1)}, u32[]{:S(2)}) copy-start(bf16[16,1,112,896]{3,2,1,0:T(8,128)(2,1)} %get-tuple-element.31) | copy-start | bytes 9633796
  173.4 5.9 %collective-permute-start.14 = (bf16[1792,256]{1,0:T(8,128)(2,1)S(1)}, bf16[1792,256]{1,0:T(8,128)(2,1)S(1)}, u32[]{:S(2)}, u32[]{:S(2)}) collective-permute-start(bf16[1792,256]{1,0:T(8,128)(2,1)S(1)} %convolution_convert_fusion), channel_id=1, source_target_pairs={{0,1},{1,0},{2,3},{3,2},{4,5},{5,4},{6,7},{7,6},{8,9},{9,8},{10,11... | collective-permute-start | bytes 2752520 | tf_op jit(solution)/shard_map/ppermute | solution.py:14
Sparse Core Ops, SparseCore 0:
  15.4 55.3 all-gather.3
  74.5 34.6 all-gather.5

commit v2 on v1

--- a/solution.py
+++ b/solution.py
@@ -83,22 +83,25 @@
     near_rotated = lax.all_gather(mine, "z", axis=0)
 
     far_grads = swap(near_grads, "core")
-    near = dot(near_grads, basis_out).astype(BF16)
-    far = dot(far_grads, basis_out).astype(BF16)
-    pieces = jnp.concatenate([near, far], axis=0)
-    summed = scatter_sum(pieces.reshape(8, 96, 896), TOK).astype(BF16)
+    near = dot(near_grads, basis_out).astype(BF16).reshape(8, 48, 896)
+    far = dot(far_grads, basis_out).astype(BF16).reshape(8, 48, 896)
+    pieces = jnp.stack([near, far], axis=1).reshape(8, 96, 896)
+    summed = scatter_sum(pieces, TOK).astype(BF16)
     grad = direct_gather(summed)
+
     near_rotated, _ = lax.optimization_barrier((near_rotated, summed))
-    near_rotated = near_rotated[:, :56].reshape(448, 1024)
-
+    near_rotated = near_rotated[:, :56].reshape(4, 2, 56, 1024)
+    near_rotated = jnp.where(ylo == 0, near_rotated, near_rotated[:, ::-1])
+    near_rotated = roll_blocks(near_rotated, x).reshape(448, 1024)
     rotated = jnp.concatenate([near_rotated, swap(near_rotated, "core")], axis=0)
-    train = rotated.reshape(2, 8, 56, 1024)[:, :, 48:].reshape(2, 64, 1024)
-    train = jnp.where(core == 0, train, train[::-1]).reshape(128, 1024)
-    rotated = rotated.reshape(4, 2, 112, 1024)
-    rotated = jnp.where(ylo == 0, rotated, rotated[:, ::-1])
-    rotated = roll_blocks(rotated, x).reshape(896, 1024)
+    train = rotated.reshape(2, 4, 2, 56, 1024)[:, :, :, 48:]
+    train = jnp.where(core == 0, train, train[::-1])
+    train = jnp.where(ylo == 0, train, train[:, :, ::-1])
+    train = roll_blocks(train.swapaxes(0, 1), (4 - x) % 4).swapaxes(0, 1)
+    train = train.reshape(128, 1024)
     grad, rotated, train = lax.optimization_barrier((grad, rotated, train))
-    grad = jnp.pad(grad.reshape(16, 48, 896), ((0, 0), (0, 8), (0, 0)))
+    grad = grad.reshape(8, 2, 48, 896).swapaxes(0, 1).reshape(16, 48, 896)
+    grad = jnp.pad(grad, ((0, 0), (0, 8), (0, 0)))
     row = jnp.arange(56)
     of_query = (row // 12 % 2)[None, :] == jnp.arange(2)[:, None]
     grad = jnp.where(of_query[:, None, :, None], grad[None], 0).reshape(2, 896, 896)

time: 221 us -> 219 us (level)
  transfers between devices with their start and end apart: 18 -> 18, of which waited for: 9 -> 9; matrix products, arithmetic and copies ran while one was open for 12% -> 13% of each run, Pallas kernels for 0% -> 0%
where the time goes in v2:
time: 219 us
  blocking collectives  80.7 us (37%)
  waiting for transfers between devices  39.7 us (18%)
  starting transfers between devices  36.6 us (17%)
  matrix products  26.6 us (12%)
  local copies, waits for them, and re-layouts  16.2 us (7%)
  between operations  13.8 us (6%)
  other arithmetic  4.97 us (2%)
    all_to_all x4, blocking collectives, exchange(): return lax.all_to_all(pieces, axes, 0, 0)  80.7 us
    ppermute x8, starting transfers between devices, swap(): return lax.ppermute(array, axis, [(0, 1), (1, 0)])  23.4 us
    all_to_all x1, waiting for transfers between devices, exchange(): return lax.all_to_all(pieces, axes, 0, 0)  21.2 us
    dot_general x8, matrix products, per_device(): dot = lambda a, b: jnp.dot(a, b, preferred_element_type=F32)  18.2 us
    ppermute x8, waiting for transfers between devices, swap(): return lax.ppermute(array, axis, [(0, 1), (1, 0)])  11.5 us
    dot_general x1, matrix products, per_device(): jnp.einsum('qed,kd->eqk', precond.astype(BF16), train, preferred_element_...  8.36 us
    ppermute x7, starting transfers between devices, direct_gather(): blocks[i, j] = lax.ppermute(own, TOK, pairs)  8.23 us
    dynamic_slice x1, local copies, waits for them, and re-layouts, pick(): return lax.dynamic_index_in_dim(array, index, axis, keepdims=False)  6.09 us
  transfers between devices with their start and end apart: 18, of which 9 were waited for; matrix products, arithmetic and copies ran while one was open for 13% of the time, Pallas kernels for 0%

profile of v2, /device:TPU:1, one launch (start us, length us, event | category | flops | bytes accessed | tf_op | source)
XLA Modules:
  0.0 218.5 jit_solution(16981007949588617728)
XLA Ops:
  6.5 1.0 copy.13
  7.6 3.8 %collective-permute-start = (bf16[24,3584]{1,0:T(8,128)(2,1)S(1)}, bf16[24,3584]{1,0:T(8,128)(2,1)S(1)}, u32[]{:S(2)}, u32[]{:S(2)}) collective-permute-start(bf16[24,3584]{1,0:T(8,128)(2,1)S(1)} %reshape.108), channel_id=1, source_target_pairs={{0,2},{2,0},{1,3},{3,1},{4,6},{6,4},{5,7},{7,5},{8,10},{10,8},{9,1... | collective-permute-start | bytes 516104 | tf_op jit(solution)/shard_map/ppermute | solution.py:14
  11.4 1.4 copy.14
  12.8 0.2 copy.15
  13.2 0.1 copy.17
  13.3 0.3 fusion.34
  13.6 0.3 fusion.30
  13.9 0.6 collective-permute-done
  14.5 0.8 pad_maximum_fusion.3
  15.4 3.5 %collective-permute-start.2 = (f32[448,512]{1,0:T(8,128)S(1)}, f32[448,512]{1,0:T(8,128)}, u32[]{:S(2)}, u32[]{:S(2)}) collective-permute-start(f32[448,512]{1,0:T(8,128)S(1)} %fusion.34), channel_id=1, source_target_pairs={{0,1},{1,0},{2,3},{3,2},{4,5},{5,4},{6,7},{7,6},{8,9},{9,8},{10,11... | collective-permute-start | bytes 2752520 | tf_op jit(solution)/shard_map/ppermute | solution.py:14
  18.8 0.1 collective-permute-start.1
  18.9 2.1 collective-permute-done.2
  21.0 1.5 add_convert_fusion.1
  22.5 2.0 collective-permute-start.3
  24.5 0.3 fusion.28
  24.8 6.1 %constant_dynamic-slice_fusion = (bf16[16,1,112,896]{3,2,1,0:T(8,128)(2,1)}, bf16[16,1,112,896]{3,2,1,0:T(8,128)(2,1)}) fusion(bf16[16,2,112,896]{3,2,1,0:T(8,128)(2,1)} %bitcast.84, s32[]{:T(128)S(6)} %select_n.105, s32[]{:T(128)S(6)} %select_n.102), kind=kLoop, calls=%fused_computation.60 | loop fusion | bytes 12845064 | tf_op jit(solution)/shard_map/jit(dynamic_index_in_dim)/dynamic_slice | solution.py:18
  30.9 5.0 %collective-permute-done.3 = bf16[448,512]{1,0:T(8,128)(2,1)S(1)} collective-permute-done((bf16[448,512]{1,0:T(8,128)(2,1)S(1)}, bf16[448,512]{1,0:T(8,128)(2,1)S(1)}, u32[]{:S(2)}, u32[]{:S(2)}) %collective-permute-start.3) | collective-permute-done | bytes 458784 | tf_op jit(solution)/shard_map/ppermute | solution.py:14
  35.8 1.5 convert_add_fusion
  37.3 27.0 %all_to_all.25 = bf16[8,56,512]{2,1,0:T(8,128)(2,1)S(1)} all-to-all(bf16[8,56,512]{2,1,0:T(8,128)(2,1)S(1)} %bitcast.99), channel_id=1, replica_groups=mesh['x'=4,'ylo'=2,'z'=8,'yhi'=2,'core'=2] {'z'}, dimensions={0} | all-to-all | bytes 917504 | tf_op jit(solution)/shard_map/all_to_all | solution.py:22
  64.3 0.1 reduce_sum.48
  64.4 3.3 %collective-permute-start.4 = (bf16[56,512]{1,0:T(8,128)(2,1)S(1)}, bf16[56,512]{1,0:T(8,128)(2,1)S(1)}, u32[]{:S(2)}, u32[]{:S(2)}) collective-permute-start(bf16[56,512]{1,0:T(8,128)(2,1)S(1)} %reduce_sum.48), channel_id=1, source_target_pairs={{0,2},{2,0},{1,3},{3,1},{4,6},{6,4},{5,7},{7,5},{8,10},{10,8},{9,1... | collective-permute-start | bytes 172040 | tf_op jit(solution)/shard_map/ppermute | solution.py:14
  67.7 1.6 collective-permute-done.4
  69.3 1.5 all-gather.4.cloned.1.call-done
  70.8 2.8 %collective-permute-start.5 = (bf16[384,3584]{1,0:T(8,128)(2,1)}, bf16[384,3584]{1,0:T(8,128)(2,1)}, u32[]{:S(2)}, u32[]{:S(2)}) collective-permute-start(bf16[384,3584]{1,0:T(8,128)(2,1)} %all-gather.4.cloned.1.call-done), channel_id=1, source_target_pairs={{0,1},{1,0},{2,3},{3,2},{4,5},{5,4},{6,7},{7,6},{8,9},{9,8},{10,11... | collective-permute-start | bytes 8257544 | tf_op jit(solution)/shard_map/ppermute | solution.py:14
  73.7 0.7 concatenate.24
  74.4 6.8 %convolution_convert_fusion.2 = bf16[384,896]{1,0:T(8,128)(2,1)S(1)} fusion(bf16[384,3584]{1,0:T(8,128)(2,1)} %all-gather.4.cloned.1.call-done, bf16[3584,896]{1,0:T(8,128)(2,1)} %param.10), kind=kOutput, calls=%fused_computation.16 | convolution fusion | flops 2466594816 | bytes 9863168 | tf_op jit(solution)/shard_map/dot_general | solution.py:63
  81.2 4.8 %convolution_convert_fusion.1 = bf16[384,896]{1,0:T(8,128)(2,1)S(1)} fusion(bf16[384,3584]{1,0:T(8,128)(2,1)} %collective-permute-done.5, bf16[3584,896]{1,0:T(8,128)(2,1)S(1)} %bitcast.86), kind=kOutput, calls=%fused_computation.15 | convolution fusion | flops 2466594816 | bytes 9863168 | tf_op jit(solution)/shard_map/dot_general | solution.py:63
  86.0 1.2 pad_maximum_fusion.1
  87.2 4.9 %all-to-all-start.1 = ((bf16[8,96,896]{2,1,0:T(8,128)(2,1)}), bf16[8,96,896]{2,1,0:T(8,128)(2,1)S(1)}, u32[]{:S(2)}, u32[]{:S(2)}) async-start(bf16[8,96,896]{2,1,0:T(8,128)(2,1)} %bitcast.15), calls=%async_computation.1 | async-start | bytes 2752512 | tf_op jit(solution)/shard_map/all_to_all | solution.py:22
  92.1 0.1 broadcast_in_dim.39
  92.3 21.2 %all-to-all-done.1 = bf16[8,96,896]{2,1,0:T(8,128)(2,1)S(1)} async-done(((bf16[8,96,896]{2,1,0:T(8,128)(2,1)}), bf16[8,96,896]{2,1,0:T(8,128)(2,1)S(1)}, u32[]{:S(2)}, u32[]{:S(2)}) %all-to-all-start.1) | async-done | bytes 1376288 | tf_op jit(solution)/shard_map/all_to_all | solution.py:22
  113.4 0.2 reduce_sum.49
  113.6 0.7 collective-permute-start.6
  114.3 1.2 collective-permute-start.8
  115.5 2.6 %collective-permute-start.9 = (bf16[96,896]{1,0:T(8,128)(2,1)S(1)}, bf16[96,896]{1,0:T(8,128)(2,1)S(1)}, u32[]{:S(2)}, u32[]{:S(2)}) collective-permute-start(bf16[96,896]{1,0:T(8,128)(2,1)S(1)} %reduce_sum.49), channel_id=1, source_target_pairs={{128,0},{160,32},{192,64},{224,96},{0,128},{32,160},{64,192},{96,2... | collective-permute-start | bytes 516104 | tf_op jit(solution)/shard_map/ppermute | solution.py:39
  118.2 0.3 collective-permute-start.10
  118.5 1.2 slice.6
  119.8 0.2 reverse_select_fusion
  120.0 0.3 fusion.24
  120.4 1.3 collective-permute-start.11
  121.7 2.1 collective-permute-start.12
  123.8 4.0 %collective-permute-start.13 = (bf16[448,1024]{1,0:T(8,128)(2,1)S(1)}, bf16[448,1024]{1,0:T(8,128)(2,1)S(1)}, u32[]{:S(2)}, u32[]{:S(2)}) collective-permute-start(bf16[448,1024]{1,0:T(8,128)(2,1)S(1)} %bitcast.93), channel_id=1, source_target_pairs={{0,1},{1,0},{2,3},{3,2},{4,5},{5,4},{6,7},{7,6},{8,9},{9,8},{10,11... | collective-permute-start | bytes 2752520 | tf_op jit(solution)/shard_map/ppermute | solution.py:14
  127.9 1.9 collective-permute-done.11
  129.8 3.6 %collective-permute-done.12 = bf16[96,896]{1,0:T(8,128)(2,1)S(1)} collective-permute-done((bf16[96,896]{1,0:T(8,128)(2,1)S(1)}, bf16[96,896]{1,0:T(8,128)(2,1)S(1)}, u32[]{:S(2)}, u32[]{:S(2)}) %collective-permute-start.12) | collective-permute-done | bytes 172064 | tf_op jit(solution)/shard_map/ppermute | solution.py:39
  133.4 0.1 pad_maximum_fusion
  133.7 0.1 fusion.25
  133.7 0.1 fusion.26
  133.9 0.1 copy.20
  134.0 0.9 copy-done.2
  134.9 0.1 pad.5
  135.0 2.4 %copy.21 = bf16[896,896]{0,1:T(8,128)(2,1)} copy(bf16[896,896]{1,0:T(8,128)(2,1)S(1)} %bitcast.87) | data formatting | bytes 3211264 | tf_op jit(solution)/shard_map/jit(_where)/broadcast_in_dim | solution.py:107
  137.4 8.4 %fusion.19 = bf16[896,2,128]{0,2,1:T(8,128)(2,1)S(1)} fusion(f32[896,1024]{1,0:T(8,128)} %param.11, pred[2,896]{1,0:T(4,128)(4,1)S(1)} %broadcast_in_dim.39, bf16[896,1024]{1,0:T(8,128)(2,1)} %copy-done.2, bf16[896,896]{0,1:T(8,128)(2,1)} %copy.21, bf16[128,1024]{1,0:T(8,128)(2,1)S(1)} %bitcast.109), kind=kOutput, calls=%fused_computation.18 | convolution fusion | flops 3765436416 | bytes 7833344 | tf_op jit(solution)/shard_map/qed,kd->eqk/dot_general | solution.py:111
  145.8 0.6 reshape.128
  146.3 0.3 copy.23
  146.7 11.9 %all_to_all.26 = bf16[8,112,256]{2,1,0:T(8,128)(2,1)S(1)} all-to-all(bf16[8,112,256]{2,1,0:T(8,128)(2,1)S(1)} %copy.23), channel_id=1, replica_groups=mesh['x'=4,'ylo'=2,'z'=8,'yhi'=2,'core'=2] {'x','ylo'}, dimensions={0} | all-to-all | bytes 917504 | tf_op jit(solution)/shard_map/all_to_all | solution.py:22
  158.6 0.1 reduce_sum.50
  158.7 9.8 %all_to_all.27 = bf16[8,112,256]{2,1,0:T(8,128)(2,1)S(1)} all-to-all(bf16[8,112,256]{2,1,0:T(8,128)(2,1)S(1)} %broadcast_in_dim.44), channel_id=1, replica_groups=mesh['x'=4,'ylo'=2,'z'=8,'yhi'=2,'core'=2] {'x','ylo'}, dimensions={0} | all-to-all | bytes 917504 | tf_op jit(solution)/shard_map/all_to_all | solution.py:22
  168.5 3.2 %convolution_convert_fusion = bf16[1792,256]{1,0:T(8,128)(2,1)S(1)} fusion(bf16[1792,896]{1,0:T(8,128)(2,1)} %bitcast.97, bf16[896,256]{1,0:T(8,128)(2,1)S(1)} %bitcast.107), kind=kOutput, calls=%fused_computation.5 | convolution fusion | flops 822542336 | bytes 4587520 | tf_op jit(solution)/shard_map/dot_general | solution.py:63
  171.7 4.0 %collective-permute-start.14 = (bf16[1792,256]{1,0:T(8,128)(2,1)S(1)}, bf16[1792,256]{1,0:T(8,128)(2,1)S(1)}, u32[]{:S(2)}, u32[]{:S(2)}) collective-permute-start(bf16[1792,256]{1,0:T(8,128)(2,1)S(1)} %convolution_convert_fusion), channel_id=1, source_target_pairs={{0,1},{1,0},{2,3},{3,2},{4,5},{5,4},{6,7},{7,6},{8,9},{9,8},{10,11... | collective-permute-start | bytes 2752520 | tf_op jit(solution)/shard_map/ppermute | solution.py:14
  175.7 2.1 collective-permute-done.14
  177.8 1.2 add_convert_fusion
  179.0 32.0 %all_to_all.28 = bf16[16,112,256]{2,1,0:T(8,128)(2,1)S(1)} all-to-all(bf16[16,112,256]{2,1,0:T(8,128)(2,1)S(1)} %bitcast.103), channel_id=1, replica_groups=mesh['x'=4,'ylo'=2,'z'=8,'yhi'=2,'core'=2] {'z','yhi'}, dimensions={0} | all-to-all | bytes 1835008 | tf_op jit(solution)/shard_map/all_to_all | solution.py:22
  210.9 0.1 reduce_sum.51
  211.1 0.6 reshape.124
  (46 shorter events, 0.6 us)
Async XLA Ops:
  6.5 6.7 %copy-start = (bf16[256,1024]{1,0:T(8,128)(2,1)S(1)}, bf16[256,1024]{1,0:T(8,128)(2,1)}, u32[]{:S(2)}) copy-start(bf16[256,1024]{1,0:T(8,128)(2,1)} %param.9) | copy-start | bytes 1572868
  6.5 6.5 %copy-start.3 = (bf16[128,256]{1,0:T(8,128)(2,1)S(1)}, bf16[128,256]{1,0:T(8,128)(2,1)}, u32[]{:S(2)}) copy-start(bf16[128,256]{1,0:T(8,128)(2,1)} %param.8) | copy-start | bytes 196612
  6.5 64.3 %all-gather.4.cloned.1.call-start = ((), (), s32[]{:S(2)}) async-start(), calls=%async_computation.5 | async-start | bytes 3096576 | tf_op jit(solution)/shard_map/all_gather | solution.py:70
  7.6 6.9 %collective-permute-start = (bf16[24,3584]{1,0:T(8,128)(2,1)S(1)}, bf16[24,3584]{1,0:T(8,128)(2,1)S(1)}, u32[]{:S(2)}, u32[]{:S(2)}) collective-permute-start(bf16[24,3584]{1,0:T(8,128)(2,1)S(1)} %reshape.108), channel_id=1, source_target_pairs={{0,2},{2,0},{1,3},{3,1},{4,6},{6,4},{5,7},{7,5},{8,10},{10,8},{9,1... | collective-permute-start | bytes 516104 | tf_op jit(solution)/shard_map/ppermute | solution.py:14
  15.3 103.2 %all-gather.6.cloned.1.call-start = ((), (), s32[]{:S(2)}) async-start(), calls=%async_computation.6 | async-start | bytes 1769472 | tf_op jit(solution)/shard_map/all_gather | solution.py:83
  15.4 5.7 %collective-permute-start.2 = (f32[448,512]{1,0:T(8,128)S(1)}, f32[448,512]{1,0:T(8,128)}, u32[]{:S(2)}, u32[]{:S(2)}) collective-permute-start(f32[448,512]{1,0:T(8,128)S(1)} %fusion.34), channel_id=1, source_target_pairs={{0,1},{1,0},{2,3},{3,2},{4,5},{5,4},{6,7},{7,6},{8,9},{9,8},{10,11... | collective-permute-start | bytes 2752520 | tf_op jit(solution)/shard_map/ppermute | solution.py:14
  18.8 12.0 %collective-permute-start.1 = (f32[448,512]{1,0:T(8,128)S(1)}, f32[448,512]{1,0:T(8,128)}, u32[]{:S(2)}, u32[]{:S(2)}) collective-permute-start(f32[448,512]{1,0:T(8,128)S(1)} %fusion.30), channel_id=1, source_target_pairs={{0,1},{1,0},{2,3},{3,2},{4,5},{5,4},{6,7},{7,6},{8,9},{9,8},{10,11... | collective-permute-start | bytes 2752520 | tf_op jit(solution)/shard_map/ppermute | solution.py:14
  22.5 13.3 %collective-permute-start.3 = (bf16[448,512]{1,0:T(8,128)(2,1)S(1)}, bf16[448,512]{1,0:T(8,128)(2,1)S(1)}, u32[]{:S(2)}, u32[]{:S(2)}) collective-permute-start(bf16[448,512]{1,0:T(8,128)(2,1)S(1)} %add_convert_fusion.1), channel_id=1, source_target_pairs={{0,2},{2,0},{1,3},{3,1},{4,6},{6,4},{5,7},{7,5},{8,10},{10,8},{9,1... | collective-permute-start | bytes 1376264 | tf_op jit(solution)/shard_map/ppermute | solution.py:14
  64.4 4.9 %collective-permute-start.4 = (bf16[56,512]{1,0:T(8,128)(2,1)S(1)}, bf16[56,512]{1,0:T(8,128)(2,1)S(1)}, u32[]{:S(2)}, u32[]{:S(2)}) collective-permute-start(bf16[56,512]{1,0:T(8,128)(2,1)S(1)} %reduce_sum.48), channel_id=1, source_target_pairs={{0,2},{2,0},{1,3},{3,1},{4,6},{6,4},{5,7},{7,5},{8,10},{10,8},{9,1... | collective-permute-start | bytes 172040 | tf_op jit(solution)/shard_map/ppermute | solution.py:14
  69.3 11.9 %slice-start = ((s8[6422528]{0:T(1024)(128)(4,1)}), s8[2228224]{0:T(1024)(128)(4,1)S(1)}, s32[]{:S(2)}) async-start(s8[6422528]{0:T(1024)(128)(4,1)} %bitcast.85), calls=%async_computation.7 | async-start | bytes 4456448
  70.8 10.3 %collective-permute-start.5 = (bf16[384,3584]{1,0:T(8,128)(2,1)}, bf16[384,3584]{1,0:T(8,128)(2,1)}, u32[]{:S(2)}, u32[]{:S(2)}) collective-permute-start(bf16[384,3584]{1,0:T(8,128)(2,1)} %all-gather.4.cloned.1.call-done), channel_id=1, source_target_pairs={{0,1},{1,0},{2,3},{3,2},{4,5},{5,4},{6,7},{7,6},{8,9},{9,8},{10,11... | collective-permute-start | bytes 8257544 | tf_op jit(solution)/shard_map/ppermute | solution.py:14
  74.4 6.8 %slice-start.1 = ((s8[6422528]{0:T(1024)(128)(4,1)}), s8[4194304]{0:T(1024)(128)(4,1)S(1)}, s32[]{:S(2)}) async-start(s8[6422528]{0:T(1024)(128)(4,1)} %bitcast.85), calls=%async_computation.8 | async-start | bytes 8388608
  87.2 26.2 %all-to-all-start.1 = ((bf16[8,96,896]{2,1,0:T(8,128)(2,1)}), bf16[8,96,896]{2,1,0:T(8,128)(2,1)S(1)}, u32[]{:S(2)}, u32[]{:S(2)}) async-start(bf16[8,96,896]{2,1,0:T(8,128)(2,1)} %bitcast.15), calls=%async_computation.1 | async-start | bytes 2752512 | tf_op jit(solution)/shard_map/all_to_all | solution.py:22
  113.6 6.7 %collective-permute-start.6 = (bf16[96,896]{1,0:T(8,128)(2,1)S(1)}, bf16[96,896]{1,0:T(8,128)(2,1)S(1)}, u32[]{:S(2)}, u32[]{:S(2)}) collective-permute-start(bf16[96,896]{1,0:T(8,128)(2,1)S(1)} %reduce_sum.49), channel_id=1, source_target_pairs={{32,0},{0,32},{96,64},{64,96},{160,128},{128,160},{224,192},{192,2... | collective-permute-start | bytes 516104 | tf_op jit(solution)/shard_map/ppermute | solution.py:39
  114.3 7.3 %collective-permute-start.7 = (bf16[96,896]{1,0:T(8,128)(2,1)S(1)}, bf16[96,896]{1,0:T(8,128)(2,1)S(1)}, u32[]{:S(2)}, u32[]{:S(2)}) collective-permute-start(bf16[96,896]{1,0:T(8,128)(2,1)S(1)} %reduce_sum.49), channel_id=1, source_target_pairs={{64,0},{96,32},{128,64},{160,96},{192,128},{224,160},{0,192},{32,2... | collective-permute-start | bytes 516104 | tf_op jit(solution)/shard_map/ppermute | solution.py:39
  114.3 9.5 %collective-permute-start.8 = (bf16[96,896]{1,0:T(8,128)(2,1)S(1)}, bf16[96,896]{1,0:T(8,128)(2,1)S(1)}, u32[]{:S(2)}, u32[]{:S(2)}) collective-permute-start(bf16[96,896]{1,0:T(8,128)(2,1)S(1)} %reduce_sum.49), channel_id=1, source_target_pairs={{96,0},{64,32},{160,64},{128,96},{224,128},{192,160},{32,192},{0,2... | collective-permute-start | bytes 516104 | tf_op jit(solution)/shard_map/ppermute | solution.py:39
  115.5 12.3 %collective-permute-start.9 = (bf16[96,896]{1,0:T(8,128)(2,1)S(1)}, bf16[96,896]{1,0:T(8,128)(2,1)S(1)}, u32[]{:S(2)}, u32[]{:S(2)}) collective-permute-start(bf16[96,896]{1,0:T(8,128)(2,1)S(1)} %reduce_sum.49), channel_id=1, source_target_pairs={{128,0},{160,32},{192,64},{224,96},{0,128},{32,160},{64,192},{96,2... | collective-permute-start | bytes 516104 | tf_op jit(solution)/shard_map/ppermute | solution.py:39
  118.2 9.7 %collective-permute-start.10 = (bf16[96,896]{1,0:T(8,128)(2,1)S(1)}, bf16[96,896]{1,0:T(8,128)(2,1)S(1)}, u32[]{:S(2)}, u32[]{:S(2)}) collective-permute-start(bf16[96,896]{1,0:T(8,128)(2,1)S(1)} %reduce_sum.49), channel_id=1, source_target_pairs={{160,0},{128,32},{224,64},{192,96},{32,128},{0,160},{96,192},{64,2... | collective-permute-start | bytes 516104 | tf_op jit(solution)/shard_map/ppermute | solution.py:39
  120.4 9.4 %collective-permute-start.11 = (bf16[96,896]{1,0:T(8,128)(2,1)S(1)}, bf16[96,896]{1,0:T(8,128)(2,1)S(1)}, u32[]{:S(2)}, u32[]{:S(2)}) collective-permute-start(bf16[96,896]{1,0:T(8,128)(2,1)S(1)} %reduce_sum.49), channel_id=1, source_target_pairs={{192,0},{224,32},{0,64},{32,96},{64,128},{96,160},{128,192},{160,2... | collective-permute-start | bytes 516104 | tf_op jit(solution)/shard_map/ppermute | solution.py:39
  121.7 11.7 %collective-permute-start.12 = (bf16[96,896]{1,0:T(8,128)(2,1)S(1)}, bf16[96,896]{1,0:T(8,128)(2,1)S(1)}, u32[]{:S(2)}, u32[]{:S(2)}) collective-permute-start(bf16[96,896]{1,0:T(8,128)(2,1)S(1)} %reduce_sum.49), channel_id=1, source_target_pairs={{224,0},{192,32},{32,64},{0,96},{96,128},{64,160},{160,192},{128,2... | collective-permute-start | bytes 516104 | tf_op jit(solution)/shard_map/ppermute | solution.py:39
  123.8 9.6 %collective-permute-start.13 = (bf16[448,1024]{1,0:T(8,128)(2,1)S(1)}, bf16[448,1024]{1,0:T(8,128)(2,1)S(1)}, u32[]{:S(2)}, u32[]{:S(2)}) collective-permute-start(bf16[448,1024]{1,0:T(8,128)(2,1)S(1)} %bitcast.93), channel_id=1, source_target_pairs={{0,1},{1,0},{2,3},{3,2},{4,5},{5,4},{6,7},{7,6},{8,9},{9,8},{10,11... | collective-permute-start | bytes 2752520 | tf_op jit(solution)/shard_map/ppermute | solution.py:14
  133.6 1.3 copy-start.2
  168.5 9.3 %copy-start.1 = (bf16[16,1,112,896]{3,2,1,0:T(8,128)(2,1)S(1)}, bf16[16,1,112,896]{3,2,1,0:T(8,128)(2,1)}, u32[]{:S(2)}) copy-start(bf16[16,1,112,896]{3,2,1,0:T(8,128)(2,1)} %get-tuple-element.31) | copy-start | bytes 9633796
  171.7 6.1 %collective-permute-start.14 = (bf16[1792,256]{1,0:T(8,128)(2,1)S(1)}, bf16[1792,256]{1,0:T(8,128)(2,1)S(1)}, u32[]{:S(2)}, u32[]{:S(2)}) collective-permute-start(bf16[1792,256]{1,0:T(8,128)(2,1)S(1)} %convolution_convert_fusion), channel_id=1, source_target_pairs={{0,1},{1,0},{2,3},{3,2},{4,5},{5,4},{6,7},{7,6},{8,9},{9,8},{10,11... | collective-permute-start | bytes 2752520 | tf_op jit(solution)/shard_map/ppermute | solution.py:14
Sparse Core Ops, SparseCore 0:
  15.4 55.3 all-gather.3
  74.5 34.5 all-gather.5

commit v3 on v2

--- a/solution.py
+++ b/solution.py
@@ -32,7 +32,7 @@
 
 def direct_gather(own):
     blocks = {(0, 0): own}
-    for i, j in ((2, 1), (2, 0), (1, 1), (3, 1), (1, 0), (3, 0), (0, 1)):
+    for i, j in ((2, 1), (1, 1), (3, 1), (0, 1), (2, 0), (1, 0), (3, 0)):
         pairs = [
             ((a + i) % 4 * 2 + (b + j) % 2, a * 2 + b) for a in range(4) for b in range(2)
         ]

time: 219 us -> 219 us (level)
  no operation moved by 1% of the time
where the time goes in v3:
time: 219 us
  blocking collectives  80.7 us (37%)
  waiting for transfers between devices  39.7 us (18%)
  starting transfers between devices  36.6 us (17%)
  matrix products  26.6 us (12%)
  local copies, waits for them, and re-layouts  16.2 us (7%)
  between operations  13.8 us (6%)
  other arithmetic  4.97 us (2%)
    all_to_all x4, blocking collectives, exchange(): return lax.all_to_all(pieces, axes, 0, 0)  80.7 us
    ppermute x8, starting transfers between devices, swap(): return lax.ppermute(array, axis, [(0, 1), (1, 0)])  23.4 us
    all_to_all x1, waiting for transfers between devices, exchange(): return lax.all_to_all(pieces, axes, 0, 0)  21.2 us
    dot_general x8, matrix products, per_device(): dot = lambda a, b: jnp.dot(a, b, preferred_element_type=F32)  18.2 us
    ppermute x8, waiting for transfers between devices, swap(): return lax.ppermute(array, axis, [(0, 1), (1, 0)])  11.5 us
    dot_general x1, matrix products, per_device(): jnp.einsum('qed,kd->eqk', precond.astype(BF16), train, preferred_element_...  8.36 us
    ppermute x7, starting transfers between devices, direct_gather(): blocks[i, j] = lax.ppermute(own, TOK, pairs)  8.23 us
    dynamic_slice x1, local copies, waits for them, and re-layouts, pick(): return lax.dynamic_index_in_dim(array, index, axis, keepdims=False)  6.09 us
  transfers between devices with their start and end apart: 18, of which 9 were waited for; matrix products, arithmetic and copies ran while one was open for 13% of the time, Pallas kernels for 0%

profile of v3, /device:TPU:1, one launch (start us, length us, event | category | flops | bytes accessed | tf_op | source)
XLA Modules:
  0.0 218.5 jit_solution(16981007949588617728)
XLA Ops:
  6.5 1.0 copy.13
  7.6 3.8 %collective-permute-start = (bf16[24,3584]{1,0:T(8,128)(2,1)S(1)}, bf16[24,3584]{1,0:T(8,128)(2,1)S(1)}, u32[]{:S(2)}, u32[]{:S(2)}) collective-permute-start(bf16[24,3584]{1,0:T(8,128)(2,1)S(1)} %reshape.108), channel_id=1, source_target_pairs={{0,2},{2,0},{1,3},{3,1},{4,6},{6,4},{5,7},{7,5},{8,10},{10,8},{9,1... | collective-permute-start | bytes 516104 | tf_op jit(solution)/shard_map/ppermute | solution.py:14
  11.4 1.4 copy.14
  12.8 0.2 copy.15
  13.2 0.1 copy.17
  13.3 0.3 fusion.34
  13.6 0.3 fusion.30
  13.9 0.6 collective-permute-done
  14.5 0.8 pad_maximum_fusion.3
  15.4 3.5 %collective-permute-start.2 = (f32[448,512]{1,0:T(8,128)S(1)}, f32[448,512]{1,0:T(8,128)}, u32[]{:S(2)}, u32[]{:S(2)}) collective-permute-start(f32[448,512]{1,0:T(8,128)S(1)} %fusion.34), channel_id=1, source_target_pairs={{0,1},{1,0},{2,3},{3,2},{4,5},{5,4},{6,7},{7,6},{8,9},{9,8},{10,11... | collective-permute-start | bytes 2752520 | tf_op jit(solution)/shard_map/ppermute | solution.py:14
  18.8 0.1 collective-permute-start.1
  18.9 2.1 collective-permute-done.2
  21.0 1.5 add_convert_fusion.1
  22.5 2.0 collective-permute-start.3
  24.5 0.3 fusion.28
  24.8 6.1 %constant_dynamic-slice_fusion = (bf16[16,1,112,896]{3,2,1,0:T(8,128)(2,1)}, bf16[16,1,112,896]{3,2,1,0:T(8,128)(2,1)}) fusion(bf16[16,2,112,896]{3,2,1,0:T(8,128)(2,1)} %bitcast.84, s32[]{:T(128)S(6)} %select_n.105, s32[]{:T(128)S(6)} %select_n.102), kind=kLoop, calls=%fused_computation.60 | loop fusion | bytes 12845064 | tf_op jit(solution)/shard_map/jit(dynamic_index_in_dim)/dynamic_slice | solution.py:18
  30.9 5.0 %collective-permute-done.3 = bf16[448,512]{1,0:T(8,128)(2,1)S(1)} collective-permute-done((bf16[448,512]{1,0:T(8,128)(2,1)S(1)}, bf16[448,512]{1,0:T(8,128)(2,1)S(1)}, u32[]{:S(2)}, u32[]{:S(2)}) %collective-permute-start.3) | collective-permute-done | bytes 458784 | tf_op jit(solution)/shard_map/ppermute | solution.py:14
  35.8 1.5 convert_add_fusion
  37.3 27.0 %all_to_all.25 = bf16[8,56,512]{2,1,0:T(8,128)(2,1)S(1)} all-to-all(bf16[8,56,512]{2,1,0:T(8,128)(2,1)S(1)} %bitcast.99), channel_id=1, replica_groups=mesh['x'=4,'ylo'=2,'z'=8,'yhi'=2,'core'=2] {'z'}, dimensions={0} | all-to-all | bytes 917504 | tf_op jit(solution)/shard_map/all_to_all | solution.py:22
  64.3 0.1 reduce_sum.48
  64.4 3.3 %collective-permute-start.4 = (bf16[56,512]{1,0:T(8,128)(2,1)S(1)}, bf16[56,512]{1,0:T(8,128)(2,1)S(1)}, u32[]{:S(2)}, u32[]{:S(2)}) collective-permute-start(bf16[56,512]{1,0:T(8,128)(2,1)S(1)} %reduce_sum.48), channel_id=1, source_target_pairs={{0,2},{2,0},{1,3},{3,1},{4,6},{6,4},{5,7},{7,5},{8,10},{10,8},{9,1... | collective-permute-start | bytes 172040 | tf_op jit(solution)/shard_map/ppermute | solution.py:14
  67.7 1.6 collective-permute-done.4
  69.3 1.5 all-gather.4.cloned.1.call-done
  70.8 2.8 %collective-permute-start.5 = (bf16[384,3584]{1,0:T(8,128)(2,1)}, bf16[384,3584]{1,0:T(8,128)(2,1)}, u32[]{:S(2)}, u32[]{:S(2)}) collective-permute-start(bf16[384,3584]{1,0:T(8,128)(2,1)} %all-gather.4.cloned.1.call-done), channel_id=1, source_target_pairs={{0,1},{1,0},{2,3},{3,2},{4,5},{5,4},{6,7},{7,6},{8,9},{9,8},{10,11... | collective-permute-start | bytes 8257544 | tf_op jit(solution)/shard_map/ppermute | solution.py:14
  73.7 0.7 concatenate.24
  74.4 6.8 %convolution_convert_fusion.2 = bf16[384,896]{1,0:T(8,128)(2,1)S(1)} fusion(bf16[384,3584]{1,0:T(8,128)(2,1)} %all-gather.4.cloned.1.call-done, bf16[3584,896]{1,0:T(8,128)(2,1)} %param.10), kind=kOutput, calls=%fused_computation.16 | convolution fusion | flops 2466594816 | bytes 9863168 | tf_op jit(solution)/shard_map/dot_general | solution.py:63
  81.2 4.8 %convolution_convert_fusion.1 = bf16[384,896]{1,0:T(8,128)(2,1)S(1)} fusion(bf16[384,3584]{1,0:T(8,128)(2,1)} %collective-permute-done.5, bf16[3584,896]{1,0:T(8,128)(2,1)S(1)} %bitcast.86), kind=kOutput, calls=%fused_computation.15 | convolution fusion | flops 2466594816 | bytes 9863168 | tf_op jit(solution)/shard_map/dot_general | solution.py:63
  86.0 1.2 pad_maximum_fusion.1
  87.2 4.9 %all-to-all-start.1 = ((bf16[8,96,896]{2,1,0:T(8,128)(2,1)}), bf16[8,96,896]{2,1,0:T(8,128)(2,1)S(1)}, u32[]{:S(2)}, u32[]{:S(2)}) async-start(bf16[8,96,896]{2,1,0:T(8,128)(2,1)} %bitcast.15), calls=%async_computation.1 | async-start | bytes 2752512 | tf_op jit(solution)/shard_map/all_to_all | solution.py:22
  92.1 0.1 broadcast_in_dim.39
  92.3 21.2 %all-to-all-done.1 = bf16[8,96,896]{2,1,0:T(8,128)(2,1)S(1)} async-done(((bf16[8,96,896]{2,1,0:T(8,128)(2,1)}), bf16[8,96,896]{2,1,0:T(8,128)(2,1)S(1)}, u32[]{:S(2)}, u32[]{:S(2)}) %all-to-all-start.1) | async-done | bytes 1376288 | tf_op jit(solution)/shard_map/all_to_all | solution.py:22
  113.4 0.2 reduce_sum.49
  113.6 0.7 collective-permute-start.6
  114.3 1.2 collective-permute-start.8
  115.5 2.6 %collective-permute-start.9 = (bf16[96,896]{1,0:T(8,128)(2,1)S(1)}, bf16[96,896]{1,0:T(8,128)(2,1)S(1)}, u32[]{:S(2)}, u32[]{:S(2)}) collective-permute-start(bf16[96,896]{1,0:T(8,128)(2,1)S(1)} %reduce_sum.49), channel_id=1, source_target_pairs={{128,0},{160,32},{192,64},{224,96},{0,128},{32,160},{64,192},{96,2... | collective-permute-start | bytes 516104 | tf_op jit(solution)/shard_map/ppermute | solution.py:39
  118.2 0.3 collective-permute-start.10
  118.5 1.2 slice.6
  119.8 0.2 reverse_select_fusion
  120.0 0.3 fusion.24
  120.4 1.3 collective-permute-start.11
  121.7 2.1 collective-permute-start.12
  123.8 4.0 %collective-permute-start.13 = (bf16[448,1024]{1,0:T(8,128)(2,1)S(1)}, bf16[448,1024]{1,0:T(8,128)(2,1)S(1)}, u32[]{:S(2)}, u32[]{:S(2)}) collective-permute-start(bf16[448,1024]{1,0:T(8,128)(2,1)S(1)} %bitcast.93), channel_id=1, source_target_pairs={{0,1},{1,0},{2,3},{3,2},{4,5},{5,4},{6,7},{7,6},{8,9},{9,8},{10,11... | collective-permute-start | bytes 2752520 | tf_op jit(solution)/shard_map/ppermute | solution.py:14
  127.9 1.9 collective-permute-done.11
  129.8 3.6 %collective-permute-done.12 = bf16[96,896]{1,0:T(8,128)(2,1)S(1)} collective-permute-done((bf16[96,896]{1,0:T(8,128)(2,1)S(1)}, bf16[96,896]{1,0:T(8,128)(2,1)S(1)}, u32[]{:S(2)}, u32[]{:S(2)}) %collective-permute-start.12) | collective-permute-done | bytes 172064 | tf_op jit(solution)/shard_map/ppermute | solution.py:39
  133.4 0.1 pad_maximum_fusion
  133.7 0.1 fusion.25
  133.7 0.1 fusion.26
  133.9 0.1 copy.20
  134.0 0.9 copy-done.2
  134.9 0.1 pad.5
  135.0 2.4 %copy.21 = bf16[896,896]{0,1:T(8,128)(2,1)} copy(bf16[896,896]{1,0:T(8,128)(2,1)S(1)} %bitcast.87) | data formatting | bytes 3211264 | tf_op jit(solution)/shard_map/jit(_where)/broadcast_in_dim | solution.py:107
  137.4 8.4 %fusion.19 = bf16[896,2,128]{0,2,1:T(8,128)(2,1)S(1)} fusion(f32[896,1024]{1,0:T(8,128)} %param.11, pred[2,896]{1,0:T(4,128)(4,1)S(1)} %broadcast_in_dim.39, bf16[896,1024]{1,0:T(8,128)(2,1)} %copy-done.2, bf16[896,896]{0,1:T(8,128)(2,1)} %copy.21, bf16[128,1024]{1,0:T(8,128)(2,1)S(1)} %bitcast.109), kind=kOutput, calls=%fused_computation.18 | convolution fusion | flops 3765436416 | bytes 7833344 | tf_op jit(solution)/shard_map/qed,kd->eqk/dot_general | solution.py:111
  145.8 0.6 reshape.128
  146.3 0.3 copy.23
  146.7 11.9 %all_to_all.26 = bf16[8,112,256]{2,1,0:T(8,128)(2,1)S(1)} all-to-all(bf16[8,112,256]{2,1,0:T(8,128)(2,1)S(1)} %copy.23), channel_id=1, replica_groups=mesh['x'=4,'ylo'=2,'z'=8,'yhi'=2,'core'=2] {'x','ylo'}, dimensions={0} | all-to-all | bytes 917504 | tf_op jit(solution)/shard_map/all_to_all | solution.py:22
  158.6 0.1 reduce_sum.50
  158.7 9.8 %all_to_all.27 = bf16[8,112,256]{2,1,0:T(8,128)(2,1)S(1)} all-to-all(bf16[8,112,256]{2,1,0:T(8,128)(2,1)S(1)} %broadcast_in_dim.44), channel_id=1, replica_groups=mesh['x'=4,'ylo'=2,'z'=8,'yhi'=2,'core'=2] {'x','ylo'}, dimensions={0} | all-to-all | bytes 917504 | tf_op jit(solution)/shard_map/all_to_all | solution.py:22
  168.5 3.2 %convolution_convert_fusion = bf16[1792,256]{1,0:T(8,128)(2,1)S(1)} fusion(bf16[1792,896]{1,0:T(8,128)(2,1)} %bitcast.97, bf16[896,256]{1,0:T(8,128)(2,1)S(1)} %bitcast.107), kind=kOutput, calls=%fused_computation.5 | convolution fusion | flops 822542336 | bytes 4587520 | tf_op jit(solution)/shard_map/dot_general | solution.py:63
  171.7 4.0 %collective-permute-start.14 = (bf16[1792,256]{1,0:T(8,128)(2,1)S(1)}, bf16[1792,256]{1,0:T(8,128)(2,1)S(1)}, u32[]{:S(2)}, u32[]{:S(2)}) collective-permute-start(bf16[1792,256]{1,0:T(8,128)(2,1)S(1)} %convolution_convert_fusion), channel_id=1, source_target_pairs={{0,1},{1,0},{2,3},{3,2},{4,5},{5,4},{6,7},{7,6},{8,9},{9,8},{10,11... | collective-permute-start | bytes 2752520 | tf_op jit(solution)/shard_map/ppermute | solution.py:14
  175.7 2.1 collective-permute-done.14
  177.8 1.2 add_convert_fusion
  179.0 32.0 %all_to_all.28 = bf16[16,112,256]{2,1,0:T(8,128)(2,1)S(1)} all-to-all(bf16[16,112,256]{2,1,0:T(8,128)(2,1)S(1)} %bitcast.103), channel_id=1, replica_groups=mesh['x'=4,'ylo'=2,'z'=8,'yhi'=2,'core'=2] {'z','yhi'}, dimensions={0} | all-to-all | bytes 1835008 | tf_op jit(solution)/shard_map/all_to_all | solution.py:22
  210.9 0.1 reduce_sum.51
  211.1 0.6 reshape.124
  (46 shorter events, 0.6 us)
Async XLA Ops:
  6.5 6.7 %copy-start = (bf16[256,1024]{1,0:T(8,128)(2,1)S(1)}, bf16[256,1024]{1,0:T(8,128)(2,1)}, u32[]{:S(2)}) copy-start(bf16[256,1024]{1,0:T(8,128)(2,1)} %param.9) | copy-start | bytes 1572868
  6.5 6.5 %copy-start.3 = (bf16[128,256]{1,0:T(8,128)(2,1)S(1)}, bf16[128,256]{1,0:T(8,128)(2,1)}, u32[]{:S(2)}) copy-start(bf16[128,256]{1,0:T(8,128)(2,1)} %param.8) | copy-start | bytes 196612
  6.5 64.3 %all-gather.4.cloned.1.call-start = ((), (), s32[]{:S(2)}) async-start(), calls=%async_computation.5 | async-start | bytes 3096576 | tf_op jit(solution)/shard_map/all_gather | solution.py:70
  7.6 6.9 %collective-permute-start = (bf16[24,3584]{1,0:T(8,128)(2,1)S(1)}, bf16[24,3584]{1,0:T(8,128)(2,1)S(1)}, u32[]{:S(2)}, u32[]{:S(2)}) collective-permute-start(bf16[24,3584]{1,0:T(8,128)(2,1)S(1)} %reshape.108), channel_id=1, source_target_pairs={{0,2},{2,0},{1,3},{3,1},{4,6},{6,4},{5,7},{7,5},{8,10},{10,8},{9,1... | collective-permute-start | bytes 516104 | tf_op jit(solution)/shard_map/ppermute | solution.py:14
  15.3 103.2 %all-gather.6.cloned.1.call-start = ((), (), s32[]{:S(2)}) async-start(), calls=%async_computation.6 | async-start | bytes 1769472 | tf_op jit(solution)/shard_map/all_gather | solution.py:83
  15.4 5.7 %collective-permute-start.2 = (f32[448,512]{1,0:T(8,128)S(1)}, f32[448,512]{1,0:T(8,128)}, u32[]{:S(2)}, u32[]{:S(2)}) collective-permute-start(f32[448,512]{1,0:T(8,128)S(1)} %fusion.34), channel_id=1, source_target_pairs={{0,1},{1,0},{2,3},{3,2},{4,5},{5,4},{6,7},{7,6},{8,9},{9,8},{10,11... | collective-permute-start | bytes 2752520 | tf_op jit(solution)/shard_map/ppermute | solution.py:14
  18.8 12.0 %collective-permute-start.1 = (f32[448,512]{1,0:T(8,128)S(1)}, f32[448,512]{1,0:T(8,128)}, u32[]{:S(2)}, u32[]{:S(2)}) collective-permute-start(f32[448,512]{1,0:T(8,128)S(1)} %fusion.30), channel_id=1, source_target_pairs={{0,1},{1,0},{2,3},{3,2},{4,5},{5,4},{6,7},{7,6},{8,9},{9,8},{10,11... | collective-permute-start | bytes 2752520 | tf_op jit(solution)/shard_map/ppermute | solution.py:14
  22.5 13.3 %collective-permute-start.3 = (bf16[448,512]{1,0:T(8,128)(2,1)S(1)}, bf16[448,512]{1,0:T(8,128)(2,1)S(1)}, u32[]{:S(2)}, u32[]{:S(2)}) collective-permute-start(bf16[448,512]{1,0:T(8,128)(2,1)S(1)} %add_convert_fusion.1), channel_id=1, source_target_pairs={{0,2},{2,0},{1,3},{3,1},{4,6},{6,4},{5,7},{7,5},{8,10},{10,8},{9,1... | collective-permute-start | bytes 1376264 | tf_op jit(solution)/shard_map/ppermute | solution.py:14
  64.4 4.9 %collective-permute-start.4 = (bf16[56,512]{1,0:T(8,128)(2,1)S(1)}, bf16[56,512]{1,0:T(8,128)(2,1)S(1)}, u32[]{:S(2)}, u32[]{:S(2)}) collective-permute-start(bf16[56,512]{1,0:T(8,128)(2,1)S(1)} %reduce_sum.48), channel_id=1, source_target_pairs={{0,2},{2,0},{1,3},{3,1},{4,6},{6,4},{5,7},{7,5},{8,10},{10,8},{9,1... | collective-permute-start | bytes 172040 | tf_op jit(solution)/shard_map/ppermute | solution.py:14
  69.3 11.9 %slice-start = ((s8[6422528]{0:T(1024)(128)(4,1)}), s8[2228224]{0:T(1024)(128)(4,1)S(1)}, s32[]{:S(2)}) async-start(s8[6422528]{0:T(1024)(128)(4,1)} %bitcast.85), calls=%async_computation.7 | async-start | bytes 4456448
  70.8 10.3 %collective-permute-start.5 = (bf16[384,3584]{1,0:T(8,128)(2,1)}, bf16[384,3584]{1,0:T(8,128)(2,1)}, u32[]{:S(2)}, u32[]{:S(2)}) collective-permute-start(bf16[384,3584]{1,0:T(8,128)(2,1)} %all-gather.4.cloned.1.call-done), channel_id=1, source_target_pairs={{0,1},{1,0},{2,3},{3,2},{4,5},{5,4},{6,7},{7,6},{8,9},{9,8},{10,11... | collective-permute-start | bytes 8257544 | tf_op jit(solution)/shard_map/ppermute | solution.py:14
  74.4 6.8 %slice-start.1 = ((s8[6422528]{0:T(1024)(128)(4,1)}), s8[4194304]{0:T(1024)(128)(4,1)S(1)}, s32[]{:S(2)}) async-start(s8[6422528]{0:T(1024)(128)(4,1)} %bitcast.85), calls=%async_computation.8 | async-start | bytes 8388608
  87.2 26.2 %all-to-all-start.1 = ((bf16[8,96,896]{2,1,0:T(8,128)(2,1)}), bf16[8,96,896]{2,1,0:T(8,128)(2,1)S(1)}, u32[]{:S(2)}, u32[]{:S(2)}) async-start(bf16[8,96,896]{2,1,0:T(8,128)(2,1)} %bitcast.15), calls=%async_computation.1 | async-start | bytes 2752512 | tf_op jit(solution)/shard_map/all_to_all | solution.py:22
  113.6 6.7 %collective-permute-start.6 = (bf16[96,896]{1,0:T(8,128)(2,1)S(1)}, bf16[96,896]{1,0:T(8,128)(2,1)S(1)}, u32[]{:S(2)}, u32[]{:S(2)}) collective-permute-start(bf16[96,896]{1,0:T(8,128)(2,1)S(1)} %reduce_sum.49), channel_id=1, source_target_pairs={{32,0},{0,32},{96,64},{64,96},{160,128},{128,160},{224,192},{192,2... | collective-permute-start | bytes 516104 | tf_op jit(solution)/shard_map/ppermute | solution.py:39
  114.3 7.3 %collective-permute-start.7 = (bf16[96,896]{1,0:T(8,128)(2,1)S(1)}, bf16[96,896]{1,0:T(8,128)(2,1)S(1)}, u32[]{:S(2)}, u32[]{:S(2)}) collective-permute-start(bf16[96,896]{1,0:T(8,128)(2,1)S(1)} %reduce_sum.49), channel_id=1, source_target_pairs={{64,0},{96,32},{128,64},{160,96},{192,128},{224,160},{0,192},{32,2... | collective-permute-start | bytes 516104 | tf_op jit(solution)/shard_map/ppermute | solution.py:39
  114.3 9.5 %collective-permute-start.8 = (bf16[96,896]{1,0:T(8,128)(2,1)S(1)}, bf16[96,896]{1,0:T(8,128)(2,1)S(1)}, u32[]{:S(2)}, u32[]{:S(2)}) collective-permute-start(bf16[96,896]{1,0:T(8,128)(2,1)S(1)} %reduce_sum.49), channel_id=1, source_target_pairs={{96,0},{64,32},{160,64},{128,96},{224,128},{192,160},{32,192},{0,2... | collective-permute-start | bytes 516104 | tf_op jit(solution)/shard_map/ppermute | solution.py:39
  115.5 12.3 %collective-permute-start.9 = (bf16[96,896]{1,0:T(8,128)(2,1)S(1)}, bf16[96,896]{1,0:T(8,128)(2,1)S(1)}, u32[]{:S(2)}, u32[]{:S(2)}) collective-permute-start(bf16[96,896]{1,0:T(8,128)(2,1)S(1)} %reduce_sum.49), channel_id=1, source_target_pairs={{128,0},{160,32},{192,64},{224,96},{0,128},{32,160},{64,192},{96,2... | collective-permute-start | bytes 516104 | tf_op jit(solution)/shard_map/ppermute | solution.py:39
  118.2 9.7 %collective-permute-start.10 = (bf16[96,896]{1,0:T(8,128)(2,1)S(1)}, bf16[96,896]{1,0:T(8,128)(2,1)S(1)}, u32[]{:S(2)}, u32[]{:S(2)}) collective-permute-start(bf16[96,896]{1,0:T(8,128)(2,1)S(1)} %reduce_sum.49), channel_id=1, source_target_pairs={{160,0},{128,32},{224,64},{192,96},{32,128},{0,160},{96,192},{64,2... | collective-permute-start | bytes 516104 | tf_op jit(solution)/shard_map/ppermute | solution.py:39
  120.4 9.4 %collective-permute-start.11 = (bf16[96,896]{1,0:T(8,128)(2,1)S(1)}, bf16[96,896]{1,0:T(8,128)(2,1)S(1)}, u32[]{:S(2)}, u32[]{:S(2)}) collective-permute-start(bf16[96,896]{1,0:T(8,128)(2,1)S(1)} %reduce_sum.49), channel_id=1, source_target_pairs={{192,0},{224,32},{0,64},{32,96},{64,128},{96,160},{128,192},{160,2... | collective-permute-start | bytes 516104 | tf_op jit(solution)/shard_map/ppermute | solution.py:39
  121.7 11.7 %collective-permute-start.12 = (bf16[96,896]{1,0:T(8,128)(2,1)S(1)}, bf16[96,896]{1,0:T(8,128)(2,1)S(1)}, u32[]{:S(2)}, u32[]{:S(2)}) collective-permute-start(bf16[96,896]{1,0:T(8,128)(2,1)S(1)} %reduce_sum.49), channel_id=1, source_target_pairs={{224,0},{192,32},{32,64},{0,96},{96,128},{64,160},{160,192},{128,2... | collective-permute-start | bytes 516104 | tf_op jit(solution)/shard_map/ppermute | solution.py:39
  123.8 9.6 %collective-permute-start.13 = (bf16[448,1024]{1,0:T(8,128)(2,1)S(1)}, bf16[448,1024]{1,0:T(8,128)(2,1)S(1)}, u32[]{:S(2)}, u32[]{:S(2)}) collective-permute-start(bf16[448,1024]{1,0:T(8,128)(2,1)S(1)} %bitcast.93), channel_id=1, source_target_pairs={{0,1},{1,0},{2,3},{3,2},{4,5},{5,4},{6,7},{7,6},{8,9},{9,8},{10,11... | collective-permute-start | bytes 2752520 | tf_op jit(solution)/shard_map/ppermute | solution.py:14
  133.6 1.3 copy-start.2
  168.5 9.3 %copy-start.1 = (bf16[16,1,112,896]{3,2,1,0:T(8,128)(2,1)S(1)}, bf16[16,1,112,896]{3,2,1,0:T(8,128)(2,1)}, u32[]{:S(2)}) copy-start(bf16[16,1,112,896]{3,2,1,0:T(8,128)(2,1)} %get-tuple-element.31) | copy-start | bytes 9633796
  171.7 6.1 %collective-permute-start.14 = (bf16[1792,256]{1,0:T(8,128)(2,1)S(1)}, bf16[1792,256]{1,0:T(8,128)(2,1)S(1)}, u32[]{:S(2)}, u32[]{:S(2)}) collective-permute-start(bf16[1792,256]{1,0:T(8,128)(2,1)S(1)} %convolution_convert_fusion), channel_id=1, source_target_pairs={{0,1},{1,0},{2,3},{3,2},{4,5},{5,4},{6,7},{7,6},{8,9},{9,8},{10,11... | collective-permute-start | bytes 2752520 | tf_op jit(solution)/shard_map/ppermute | solution.py:14
Sparse Core Ops, SparseCore 0:
  15.4 55.3 all-gather.3
  74.5 34.5 all-gather.5
